TPU v7x, 32 devices: a whole 2x2x4 slice. The times are simulated.
32 devices in a mesh: section: 2 (over x), dp: 4 (over y, core), seq: 4 (over z).
Axes of the slice: x: 2, y: 2, z: 4, core: 2. Of those that a mesh axis runs over, the one named last changes fastest.
Arguments:
- cell_tokens: bfloat16 [8, 2048, 768], P('dp', 'seq'), may hold values from -6 to 6
- cell_lengths: int32 [8, 16], P('dp'), may hold values from 1 to 1537, as said below
- out_grad: bfloat16 [8, 2048, 768], P('dp', 'seq'), may hold values from -6 to 6
- norm1_gain: bfloat16 [2, 768], P('section'), may hold values from 0.25 to 1.75
- norm1_bias: bfloat16 [2, 768], P('section'), may hold values from -1.75 to 1.75
- qkv_weight: bfloat16 [2, 768, 2304], P('section'), may hold values from -0.21875 to 0.21875
- query_bias: bfloat16 [2, 768], P('section'), may hold values from -3 to 3
- value_bias: bfloat16 [2, 768], P('section'), may hold values from -0.625 to 0.625
- out_weight: bfloat16 [2, 768, 768], P('section'), may hold values from -1.25 to 1.25
- out_bias: bfloat16 [2, 768], P('section'), may hold values from -1.75 to 1.75
- norm2_gain: bfloat16 [2, 768], P('section'), may hold values from 0.25 to 1.75
- norm2_bias: bfloat16 [2, 768], P('section'), may hold values from -1.75 to 1.75
- in_weight: bfloat16 [2, 768, 3072], P('section'), may hold values from -0.21875 to 0.21875
- in_bias: bfloat16 [2, 3072], P('section'), may hold values from -3 to 3
- back_weight: bfloat16 [2, 3072, 768], P('section'), may hold values from -0.109375 to 0.109375
- back_bias: bfloat16 [2, 768], P('section'), may hold values from -1.75 to 1.75
Outputs:
- layer_outputs: bfloat16 [2, 8, 2048, 768], P('section', 'dp', 'seq')
- input_grads: float32 [2, 8, 2048, 768], P('section', 'dp', 'seq')
- norm1_gain_grad: float32 [2, 768], P('section', ('dp', 'seq'))
- norm1_bias_grad: float32 [2, 768], P('section', ('dp', 'seq'))
- qkv_weight_grad: float32 [2, 768, 2304], P('section', ('dp', 'seq'))
- query_bias_grad: float32 [2, 768], P('section', ('dp', 'seq'))
- value_bias_grad: float32 [2, 768], P('section', ('dp', 'seq'))
- out_weight_grad: float32 [2, 768, 768], P('section', ('dp', 'seq'))
- out_bias_grad: float32 [2, 768], P('section', ('dp', 'seq'))
- norm2_gain_grad: float32 [2, 768], P('section', ('dp', 'seq'))
- norm2_bias_grad: float32 [2, 768], P('section', ('dp', 'seq'))
- in_weight_grad: float32 [2, 768, 3072], P('section', ('dp', 'seq'))
- in_bias_grad: float32 [2, 3072], P('section', ('dp', 'seq'))
- back_weight_grad: float32 [2, 3072, 768], P('section', ('dp', 'seq'))
- back_bias_grad: float32 [2, 768], P('section', ('dp', 'seq'))
Inputs may be any that keep to these rules, and one draw needn't show every extreme that they name: `cell_lengths`: each row holds 16 cells whose lengths sum to 2048. In each group of 2 consecutive rows, one row drawn from the seed has a cell of 1537 positions that starts within the first 512 positions.
All inputs are finite; a program needn't handle non-finite values.
Results may differ from a plain program's by a relative error of at most 0.014.
Values may be sent and summed in bfloat16 or wider, within the bound.
A program may use at most 384 MiB of HBM per device.

v0:
```python
from functools import partial

import jax
import jax.numpy as jnp
from jax import lax
from jax.sharding import PartitionSpec as P

HEADS = 12


SCALE = 0.125
EPS = 1e-05
MASKED = -1e30


def from_behind(x, axis, by):
    peers = lax.axis_size(axis)
    pairs = [(i, i + by) for i in range(peers) if 0 <= i + by < peers]
    return lax.ppermute(x, axis, pairs)


def norm_rows(values, gain_vec, bias_vec):
    centre = jnp.mean(values, axis=-1, keepdims=True)
    offset = values - centre
    spread = jnp.mean(offset * offset, axis=-1, keepdims=True)
    return offset * lax.rsqrt(spread + EPS) * gain_vec + bias_vec


def row_segments(lengths, row_length):
    limits = jnp.cumsum(lengths, axis=-1)
    places = jnp.arange(row_length, dtype=jnp.int32)
    return jnp.sum((places[None, :, None] >= limits[:, None, :]).astype(jnp.int32), axis=-1)


def split_heads(values):
    return values.reshape(values.shape[0], HEADS, values.shape[1] // HEADS)


def masked_scores(queries, keys_in, seg_query, seg_keys):
    scores = (
        jnp.einsum(
            "qhe,khe->hqk",
            split_heads(queries),
            split_heads(keys_in),
            preferred_element_type=jnp.float32,
        )
        * SCALE
    )
    return jnp.where((seg_query[:, None] == seg_keys[None, :])[None], scores, MASKED)


def softmax_parts(scores):
    highest = jnp.max(scores, axis=-1)
    raised = jnp.exp(scores - highest[..., None])
    summed = jnp.sum(raised, axis=-1)
    return (raised / summed[..., None], highest, summed)


def project_in(inputs, weights):
    normed = norm_rows(inputs, weights[0], weights[1]).astype(jnp.bfloat16)
    joined = jnp.dot(normed, weights[2], preferred_element_type=jnp.float32)
    model_width = inputs.shape[1]
    queries = (joined[:, :model_width] + weights[3]).astype(jnp.bfloat16)
    keys_out = joined[:, model_width : 2 * model_width].astype(jnp.bfloat16)
    values_out = (joined[:, 2 * model_width :] + weights[4]).astype(jnp.bfloat16)
    return (normed, queries, keys_out, values_out)


def attend(queries, keys_all, values_all, seg_own, seg_row):
    soft_probs, highest, summed = softmax_parts(masked_scores(queries, keys_all, seg_own, seg_row))
    low_probs = soft_probs.astype(jnp.bfloat16)
    combined = jnp.einsum(
        "hqk,khe->qhe", low_probs, split_heads(values_all), preferred_element_type=jnp.float32
    )
    return (
        combined.reshape(queries.shape).astype(jnp.bfloat16),
        soft_probs,
        low_probs,
        highest,
        summed,
    )


def finish(inputs, attended, weights):
    resid_sum = (
        inputs + jnp.dot(attended, weights[5], preferred_element_type=jnp.float32) + weights[6]
    )
    normed = norm_rows(resid_sum, weights[7], weights[8]).astype(jnp.bfloat16)
    hidden_pre = jnp.dot(normed, weights[9], preferred_element_type=jnp.float32) + weights[10]
    active = jax.nn.gelu(hidden_pre, approximate=False).astype(jnp.bfloat16)
    result = (
        resid_sum + jnp.dot(active, weights[11], preferred_element_type=jnp.float32) + weights[12]
    )
    return (result, resid_sum, normed, hidden_pre, active)


def store_slot(buffer, item_new, slot_idx, is_valid):
    current = lax.dynamic_index_in_dim(buffer, slot_idx, 0, keepdims=False)
    return lax.dynamic_update_index_in_dim(
        buffer, jnp.where(is_valid, item_new, current), slot_idx, 0
    )


def token_sum(values):
    return jnp.sum(values.astype(jnp.float32), axis=0)


def on_device(
    cell_tokens,
    cell_lengths,
    out_grad,
    norm1_gain,
    norm1_bias,
    qkv_weight,
    query_bias,
    value_bias,
    out_weight,
    out_bias,
    norm2_gain,
    norm2_bias,
    in_weight,
    in_bias,
    back_weight,
    back_bias,
):
    raw_weights = (
        norm1_gain,
        norm1_bias,
        qkv_weight,
        query_bias,
        value_bias,
        out_weight,
        out_bias,
        norm2_gain,
        norm2_bias,
        in_weight,
        in_bias,
        back_weight,
        back_bias,
    )
    weights = tuple(
        (weight[0].astype(jnp.float32) if weight.ndim == 2 else weight[0] for weight in raw_weights)
    )
    sections = lax.axis_size("section")
    section_rank = lax.axis_index("section")
    micro_count, local_len, model_width = cell_tokens.shape
    row_length = local_len * lax.axis_size("seq")
    own_start = lax.axis_index("seq") * local_len
    segments = row_segments(cell_lengths, row_length)
    tick_count = micro_count + sections - 1
    kept_depth = 1

    def row_segs(slot_idx):
        seg_row = lax.dynamic_index_in_dim(segments, slot_idx, 0, keepdims=False)
        return (seg_row, lax.dynamic_slice_in_dim(seg_row, own_start, local_len))

    def forward_tick(tick_now, state_now):
        incoming, kept_in, outputs, kept_keys, kept_values = state_now
        index_now = tick_now - section_rank
        is_valid = (index_now >= 0) & (index_now < micro_count)
        slot_idx = jnp.clip(index_now, 0, micro_count - 1)
        first_in = lax.dynamic_index_in_dim(cell_tokens, slot_idx, 0, keepdims=False)
        layer_in = jnp.where(section_rank == 0, first_in, incoming)
        seg_row, seg_own = row_segs(slot_idx)
        inputs = layer_in.astype(jnp.float32)
        normed, queries, keys_out, values_out = project_in(inputs, weights)
        keys_all, values_all = (
            lax.all_gather(keys_out, "seq", axis=0, tiled=True),
            lax.all_gather(values_out, "seq", axis=0, tiled=True),
        )
        attended = attend(queries, keys_all, values_all, seg_own, seg_row)[0]
        result = finish(inputs, attended, weights)[0].astype(jnp.bfloat16)
        kept_in = store_slot(kept_in, layer_in, slot_idx, is_valid)
        outputs = store_slot(outputs, result, slot_idx, is_valid)
        passed = from_behind(result, "section", 1)
        return (passed, kept_in, outputs, kept_keys, kept_values)

    start_state = (
        jnp.zeros((local_len, model_width), jnp.bfloat16),
        jnp.zeros((micro_count, local_len, model_width), jnp.bfloat16),
        jnp.zeros((micro_count, local_len, model_width), jnp.bfloat16),
        jnp.zeros((kept_depth, row_length, model_width), jnp.bfloat16),
        jnp.zeros((kept_depth, row_length, model_width), jnp.bfloat16),
    )
    ignored, kept_in, outputs, kept_keys, kept_values = lax.fori_loop(
        0, tick_count, forward_tick, start_state
    )

    def backward_tick(tick_now, state_now):
        incoming, in_grads, totals = state_now
        index_now = tick_now - (sections - 1 - section_rank)
        is_valid = (index_now >= 0) & (index_now < micro_count)
        slot_idx = jnp.clip(index_now, 0, micro_count - 1)
        from_out = lax.dynamic_index_in_dim(out_grad, slot_idx, 0, keepdims=False)
        grad_out = jnp.where(section_rank == sections - 1, from_out, incoming).astype(jnp.float32)
        inputs = lax.dynamic_index_in_dim(kept_in, slot_idx, 0, keepdims=False).astype(jnp.float32)
        seg_row, seg_own = row_segs(slot_idx)
        normed_one, queries, keys_out, values_out = project_in(inputs, weights)
        keys_all, values_all = (
            lax.all_gather(keys_out, "seq", axis=0, tiled=True),
            lax.all_gather(values_out, "seq", axis=0, tiled=True),
        )
        attended, soft_probs, low_probs, highest, summed = attend(
            queries, keys_all, values_all, seg_own, seg_row
        )
        result, resid_sum, normed_two, hidden_pre, active = finish(inputs, attended, weights)
        d_result = grad_out.astype(jnp.bfloat16)
        g_back_w = jnp.einsum("tf,td->fd", active, d_result, preferred_element_type=jnp.float32)
        g_back_b = token_sum(d_result)
        d_active = jnp.einsum(
            "td,fd->tf", d_result, weights[11], preferred_element_type=jnp.float32
        )
        gelu_value, gelu_back = jax.vjp(partial(jax.nn.gelu, approximate=False), hidden_pre)
        d_hidden = gelu_back(d_active)[0].astype(jnp.bfloat16)
        g_in_w = jnp.einsum("td,tf->df", normed_two, d_hidden, preferred_element_type=jnp.float32)
        g_in_b = token_sum(d_hidden)
        d_normed_two = jnp.einsum(
            "tf,df->td", d_hidden, weights[9], preferred_element_type=jnp.float32
        )
        norm_value, norm_two_back = jax.vjp(norm_rows, resid_sum, weights[7], weights[8])
        d_resid_norm, g_gain_two, g_bias_two = norm_two_back(d_normed_two)
        d_resid = grad_out + d_resid_norm
        d_proj = d_resid.astype(jnp.bfloat16)
        g_out_w = jnp.einsum("td,te->de", attended, d_proj, preferred_element_type=jnp.float32)
        g_out_b = token_sum(d_proj)
        d_attended = jnp.einsum(
            "te,de->td", d_proj, weights[5], preferred_element_type=jnp.float32
        ).astype(jnp.bfloat16)
        dout_heads = split_heads(d_attended)
        d_probs = jnp.einsum(
            "qhe,khe->hqk", dout_heads, split_heads(values_all), preferred_element_type=jnp.float32
        )
        delta_rows = jnp.sum(soft_probs * d_probs, axis=-1)
        d_scores = (soft_probs * (d_probs - delta_rows[..., None])).astype(jnp.bfloat16)
        d_query = (
            (
                jnp.einsum(
                    "hqk,khe->qhe",
                    d_scores,
                    split_heads(keys_all),
                    preferred_element_type=jnp.float32,
                )
                * SCALE
            )
            .reshape(local_len, model_width)
            .astype(jnp.bfloat16)
        )
        key_part = (
            jnp.einsum(
                "hqk,qhe->khe", d_scores, split_heads(queries), preferred_element_type=jnp.float32
            )
            * SCALE
        ).reshape(row_length, model_width)
        value_part = jnp.einsum(
            "hqk,qhe->khe", low_probs, dout_heads, preferred_element_type=jnp.float32
        ).reshape(row_length, model_width)
        d_keys, d_values = (
            lax.psum_scatter(
                key_part.astype(jnp.bfloat16), "seq", scatter_dimension=0, tiled=True
            ).astype(jnp.float32),
            lax.psum_scatter(
                value_part.astype(jnp.bfloat16), "seq", scatter_dimension=0, tiled=True
            ).astype(jnp.float32),
        )
        d_values_low = d_values.astype(jnp.bfloat16)
        d_joined = jnp.concatenate([d_query, d_keys.astype(jnp.bfloat16), d_values_low], axis=1)
        g_qkv_w = jnp.einsum("td,tf->df", normed_one, d_joined, preferred_element_type=jnp.float32)
        g_q_b = token_sum(d_query)
        g_v_b = token_sum(d_values_low)
        d_normed_one = jnp.einsum(
            "tf,df->td", d_joined, weights[2], preferred_element_type=jnp.float32
        )
        norm_value_one, norm_one_back = jax.vjp(norm_rows, inputs, weights[0], weights[1])
        d_inputs_norm, g_gain_one, g_bias_one = norm_one_back(d_normed_one)
        d_inputs = d_resid + d_inputs_norm
        new_grads = (
            g_gain_one,
            g_bias_one,
            g_qkv_w,
            g_q_b,
            g_v_b,
            g_out_w,
            g_out_b,
            g_gain_two,
            g_bias_two,
            g_in_w,
            g_in_b,
            g_back_w,
            g_back_b,
        )
        totals = tuple(
            (
                running + jnp.where(is_valid, grad_new, 0.0)
                for running, grad_new in zip(totals, new_grads)
            )
        )
        shown = jnp.where(
            section_rank == 0, d_inputs, d_inputs.astype(jnp.bfloat16).astype(jnp.float32)
        )
        in_grads = store_slot(in_grads, shown, slot_idx, is_valid)
        passed = from_behind(d_inputs.astype(jnp.bfloat16), "section", -1)
        return (passed, in_grads, totals)

    back_state = (
        jnp.zeros((local_len, model_width), jnp.bfloat16),
        jnp.zeros((micro_count, local_len, model_width), jnp.float32),
        tuple((jnp.zeros(weight.shape, jnp.float32) for weight in weights)),
    )
    ignored_grad, in_grads, totals = lax.fori_loop(0, tick_count, backward_tick, back_state)
    reduced = lax.psum_scatter(totals, ("dp", "seq"), scatter_dimension=0, tiled=True)
    return (
        outputs[None],
        in_grads[None],
        reduced[0][None],
        reduced[1][None],
        reduced[2][None],
        reduced[3][None],
        reduced[4][None],
        reduced[5][None],
        reduced[6][None],
        reduced[7][None],
        reduced[8][None],
        reduced[9][None],
        reduced[10][None],
        reduced[11][None],
        reduced[12][None],
    )


def solution(mesh):
    in_specs = (
        P("dp", "seq", None),
        P("dp", None),
        P("dp", "seq", None),
        P("section", None),
        P("section", None),
        P("section", None, None),
        P("section", None),
        P("section", None),
        P("section", None, None),
        P("section", None),
        P("section", None),
        P("section", None),
        P("section", None, None),
        P("section", None),
        P("section", None, None),
        P("section", None),
    )
    out_specs = (
        P("section", "dp", "seq", None),
        P("section", "dp", "seq", None),
        P("section", ("dp", "seq")),
        P("section", ("dp", "seq")),
        P("section", ("dp", "seq"), None),
        P("section", ("dp", "seq")),
        P("section", ("dp", "seq")),
        P("section", ("dp", "seq"), None),
        P("section", ("dp", "seq")),
        P("section", ("dp", "seq")),
        P("section", ("dp", "seq")),
        P("section", ("dp", "seq"), None),
        P("section", ("dp", "seq")),
        P("section", ("dp", "seq"), None),
        P("section", ("dp", "seq")),
    )
    return jax.shard_map(
        on_device, mesh=mesh, in_specs=in_specs, out_specs=out_specs, check_vma=False
    )
```

profile of v0, /device:TPU:0, one launch (start us, length us, event | category | flops | bytes accessed | tf_op | source)
XLA Modules:
  0.0 2228.8 jit_solution(12750887716204382075)
XLA Ops:
  16.5 618.5 %while.65 = (s32[]{:T(128)}, bf16[512,768]{1,0:T(8,128)(2,1)S(1)}, bf16[2,512,768]{2,1,0:T(8,128)(2,1)S(1)}, bf16[2,512,768]{2,1,0:T(8,128)(2,1)}, pred[]{:T(512...) while((s32[]{:T(128)}, bf16[512,768]{1,0:T(8,128)(2,1)S(1)}, ...), condition=%wide.region_9.10_spmd, body=%wide.region_2.9_spmd.sunk | while | flops 10663103488 | bytes 253254288 | solution.py:185
  31.2 60.1 %all-gather.7.cloned.1.call-done = bf16[2048,768]{1,0:T(8,128)(2,1)} async-done(((bf16[512,768]{1,0:T(8,128)(2,1)}), bf16[2048,768]{1,0:T(8,128)(2,1)}) %all-gather.7.cloned.1.call-update) | async-done | bytes 3145744 | tf_op jit(solution)/shard_map/while/body/eval_jaxpr/all_gather | solution.py:168
  120.1 35.0 %all-gather.5.cloned.1.call-done = bf16[2048,768]{1,0:T(8,128)(2,1)} async-done(((bf16[512,768]{1,0:T(8,128)(2,1)}), bf16[2048,768]{1,0:T(8,128)(2,1)}) %all-gather.5.cloned.1.call-update) | async-done | bytes 3145744 | tf_op jit(solution)/shard_map/while/body/eval_jaxpr/all_gather | solution.py:169
  239.5 57.2 %all-gather.7.cloned.1.call-done = bf16[2048,768]{1,0:T(8,128)(2,1)} async-done(((bf16[512,768]{1,0:T(8,128)(2,1)}), bf16[2048,768]{1,0:T(8,128)(2,1)}) %all-gather.7.cloned.1.call-update) | async-done | bytes 3145744 | tf_op jit(solution)/shard_map/while/body/eval_jaxpr/all_gather | solution.py:168
  301.3 24.2 %fusion.244 = (f32[12,512]{1,0:T(8,128)S(1)}, f32[12,512,2048]{2,1,0:T(8,128)}) fusion(pred[512,2048]{1,0:T(8,128)(4,1)S(1)} %broadcast_compare_fusion.4, bf16[512,12,64]{0,2,1:T(8,128)(2,1)} %bitcast.289, bf16[2048,12,64]{0,2,1:T(8,128)(2,1)} %bitcast.282), kind=kOutput, calls=%fused_computation.237.clone.1 | convolution fusion | flops 1660946432 | bytes 55336960 | tf_op jit(solution)/shard_map/while/body/eval_jaxpr/sub | solution.py:54
  325.4 34.8 %all-gather.5.cloned.1.call-done = bf16[2048,768]{1,0:T(8,128)(2,1)} async-done(((bf16[512,768]{1,0:T(8,128)(2,1)}), bf16[2048,768]{1,0:T(8,128)(2,1)}) %all-gather.5.cloned.1.call-update) | async-done | bytes 3145744 | tf_op jit(solution)/shard_map/while/body/eval_jaxpr/all_gather | solution.py:169
  444.6 57.2 %all-gather.7.cloned.1.call-done = bf16[2048,768]{1,0:T(8,128)(2,1)} async-done(((bf16[512,768]{1,0:T(8,128)(2,1)}), bf16[2048,768]{1,0:T(8,128)(2,1)}) %all-gather.7.cloned.1.call-update) | async-done | bytes 3145744 | tf_op jit(solution)/shard_map/while/body/eval_jaxpr/all_gather | solution.py:168
  506.4 24.2 %fusion.244 = (f32[12,512]{1,0:T(8,128)S(1)}, f32[12,512,2048]{2,1,0:T(8,128)}) fusion(pred[512,2048]{1,0:T(8,128)(4,1)S(1)} %broadcast_compare_fusion.4, bf16[512,12,64]{0,2,1:T(8,128)(2,1)} %bitcast.289, bf16[2048,12,64]{0,2,1:T(8,128)(2,1)} %bitcast.282), kind=kOutput, calls=%fused_computation.237.clone.1 | convolution fusion | flops 1660946432 | bytes 55336960 | tf_op jit(solution)/shard_map/while/body/eval_jaxpr/sub | solution.py:54
  530.5 34.8 %all-gather.5.cloned.1.call-done = bf16[2048,768]{1,0:T(8,128)(2,1)} async-done(((bf16[512,768]{1,0:T(8,128)(2,1)}), bf16[2048,768]{1,0:T(8,128)(2,1)}) %all-gather.5.cloned.1.call-update) | async-done | bytes 3145744 | tf_op jit(solution)/shard_map/while/body/eval_jaxpr/all_gather | solution.py:169
  637.0 1189.4 %while.66 = (s32[]{:T(128)}, bf16[512,768]{1,0:T(8,128)(2,1)S(1)}, f32[2,512,768]{2,1,0:T(8,128)}, f32[768]{0:T(1024)}, f32[768]{0:T(1024)}, /*index=5*/f32[768,...) while((s32[]{:T(128)}, bf16[512,768]{1,0:T(8,128)(2,1)S(1)}, ...), condition=%wide.region_33.34_spmd.clone, body=%wide.region_10.33_spmd.clone.sunk | while | flops 29386102784 | bytes 982418496 | solution.py:309
  654.3 54.5 %all-gather.11.cloned.1.call-done = bf16[2048,768]{1,0:T(8,128)(2,1)} async-done(((bf16[512,768]{1,0:T(8,128)(2,1)}), bf16[2048,768]{1,0:T(8,128)(2,1)}) %all-gather.11.cloned.1.call-update) | async-done | bytes 3145744 | tf_op jit(solution)/shard_map/while/body/eval_jaxpr/all_gather | solution.py:200
  712.1 24.8 %fusion.280 = (f32[12,512]{1,0:T(8,128)S(1)}, f32[12,512,2048]{2,1,0:T(8,128)}) fusion(pred[512,2048]{1,0:T(8,128)(4,1)} %broadcast_compare_fusion.5, bf16[512,12,64]{0,2,1:T(8,128)(2,1)} %bitcast.284, bf16[2048,12,64]{0,2,1:T(8,128)(2,1)S(1)} %bitcast.272), kind=kOutput, calls=%fused_computation.239.clone.1 | convolution fusion | flops 1660946432 | bytes 55336960 | tf_op jit(solution)/shard_map/while/body/eval_jaxpr/sub | solution.py:54
  737.0 35.6 %all-gather.9.cloned.1.call-done = bf16[2048,768]{1,0:T(8,128)(2,1)} async-done(((bf16[512,768]{1,0:T(8,128)(2,1)}), bf16[2048,768]{1,0:T(8,128)(2,1)}) %all-gather.9.cloned.1.call-update) | async-done | bytes 3145744 | tf_op jit(solution)/shard_map/while/body/eval_jaxpr/all_gather | solution.py:201
  850.8 31.6 %multiply_reduce_fusion.12 = (f32[12,512]{1,0:T(8,128)S(1)}, f32[12,512,2048]{2,1,0:T(8,128)}) fusion(f32[12,512,2048]{2,1,0:T(8,128)} %get-tuple-element.2142, f32[12,512]{1,0:T(8,128)S(1)} %get-tuple-element.2143, bf16[512,12,64]{0,2,1:T(8,128)(2,1)} %bitcast.291, bf16[2048,12,64]{0,2,1:T(8,128)(2,1)S(1)} %bitcast.281), kind=kOutput, calls=%fused_computation.105.clone.1 | convolution fusion | flops 1648355328 | bytes 104644608 | tf_op jit(solution)/shard_map/while/body/eval_jaxpr/qhe,khe->hqk/dot_general | solution.py:230
  882.5 41.3 %multiply_convert_fusion.9 = bf16[12,512,2048]{2,1,0:T(8,128)(2,1)} fusion(f32[12,512,2048]{2,1,0:T(8,128)} %get-tuple-element.2153, f32[12,512]{1,0:T(8,128)S(1)} %get-tuple-element.2154, f32[12,512,2048]{2,1,0:T(8,128)} %get-tuple-element.2142, f32[12,512]{1,0:T(8,128)S(1)} %get-tuple-element.2143), kind=kLoop, calls=%fused_computation.104.clone.1 | loop fusion | flops 50331648 | bytes 125878272 | tf_op jit(solution)/shard_map/while/body/eval_jaxpr/convert_element_type | solution.py:234
  971.2 32.7 %reduce-scatter.17.cloned.1.call-done = bf16[512,768]{0,1:T(8,128)(2,1)} async-done(((bf16[2048,768]{0,1:T(8,128)(2,1)}), bf16[512,768]{0,1:T(8,128)(2,1)}) %reduce-scatter.17.cloned.1.call-update) | async-done | bytes 786448 | tf_op jit(solution)/shard_map/while/body/eval_jaxpr/reduce_scatter | solution.py:258
  1050.4 54.1 %all-gather.11.cloned.1.call-done = bf16[2048,768]{1,0:T(8,128)(2,1)} async-done(((bf16[512,768]{1,0:T(8,128)(2,1)}), bf16[2048,768]{1,0:T(8,128)(2,1)}) %all-gather.11.cloned.1.call-update) | async-done | bytes 3145744 | tf_op jit(solution)/shard_map/while/body/eval_jaxpr/all_gather | solution.py:200
  1107.8 24.8 %fusion.280 = (f32[12,512]{1,0:T(8,128)S(1)}, f32[12,512,2048]{2,1,0:T(8,128)}) fusion(pred[512,2048]{1,0:T(8,128)(4,1)} %broadcast_compare_fusion.5, bf16[512,12,64]{0,2,1:T(8,128)(2,1)} %bitcast.284, bf16[2048,12,64]{0,2,1:T(8,128)(2,1)S(1)} %bitcast.272), kind=kOutput, calls=%fused_computation.239.clone.1 | convolution fusion | flops 1660946432 | bytes 55336960 | tf_op jit(solution)/shard_map/while/body/eval_jaxpr/sub | solution.py:54
  1132.7 35.3 %all-gather.9.cloned.1.call-done = bf16[2048,768]{1,0:T(8,128)(2,1)} async-done(((bf16[512,768]{1,0:T(8,128)(2,1)}), bf16[2048,768]{1,0:T(8,128)(2,1)}) %all-gather.9.cloned.1.call-update) | async-done | bytes 3145744 | tf_op jit(solution)/shard_map/while/body/eval_jaxpr/all_gather | solution.py:201
  1246.5 31.6 %multiply_reduce_fusion.12 = (f32[12,512]{1,0:T(8,128)S(1)}, f32[12,512,2048]{2,1,0:T(8,128)}) fusion(f32[12,512,2048]{2,1,0:T(8,128)} %get-tuple-element.2142, f32[12,512]{1,0:T(8,128)S(1)} %get-tuple-element.2143, bf16[512,12,64]{0,2,1:T(8,128)(2,1)} %bitcast.291, bf16[2048,12,64]{0,2,1:T(8,128)(2,1)S(1)} %bitcast.281), kind=kOutput, calls=%fused_computation.105.clone.1 | convolution fusion | flops 1648355328 | bytes 104644608 | tf_op jit(solution)/shard_map/while/body/eval_jaxpr/qhe,khe->hqk/dot_general | solution.py:230
  1278.2 41.0 %multiply_convert_fusion.9 = bf16[12,512,2048]{2,1,0:T(8,128)(2,1)} fusion(f32[12,512,2048]{2,1,0:T(8,128)} %get-tuple-element.2153, f32[12,512]{1,0:T(8,128)S(1)} %get-tuple-element.2154, f32[12,512,2048]{2,1,0:T(8,128)} %get-tuple-element.2142, f32[12,512]{1,0:T(8,128)S(1)} %get-tuple-element.2143), kind=kLoop, calls=%fused_computation.104.clone.1 | loop fusion | flops 50331648 | bytes 125878272 | tf_op jit(solution)/shard_map/while/body/eval_jaxpr/convert_element_type | solution.py:234
  1372.3 27.4 %reduce-scatter.17.cloned.1.call-done = bf16[512,768]{0,1:T(8,128)(2,1)} async-done(((bf16[2048,768]{0,1:T(8,128)(2,1)}), bf16[512,768]{0,1:T(8,128)(2,1)}) %reduce-scatter.17.cloned.1.call-update) | async-done | bytes 786448 | tf_op jit(solution)/shard_map/while/body/eval_jaxpr/reduce_scatter | solution.py:258
  1446.1 54.1 %all-gather.11.cloned.1.call-done = bf16[2048,768]{1,0:T(8,128)(2,1)} async-done(((bf16[512,768]{1,0:T(8,128)(2,1)}), bf16[2048,768]{1,0:T(8,128)(2,1)}) %all-gather.11.cloned.1.call-update) | async-done | bytes 3145744 | tf_op jit(solution)/shard_map/while/body/eval_jaxpr/all_gather | solution.py:200
  1503.8 24.8 %fusion.280 = (f32[12,512]{1,0:T(8,128)S(1)}, f32[12,512,2048]{2,1,0:T(8,128)}) fusion(pred[512,2048]{1,0:T(8,128)(4,1)} %broadcast_compare_fusion.5, bf16[512,12,64]{0,2,1:T(8,128)(2,1)} %bitcast.284, bf16[2048,12,64]{0,2,1:T(8,128)(2,1)S(1)} %bitcast.272), kind=kOutput, calls=%fused_computation.239.clone.1 | convolution fusion | flops 1660946432 | bytes 55336960 | tf_op jit(solution)/shard_map/while/body/eval_jaxpr/sub | solution.py:54
  1528.7 35.1 %all-gather.9.cloned.1.call-done = bf16[2048,768]{1,0:T(8,128)(2,1)} async-done(((bf16[512,768]{1,0:T(8,128)(2,1)}), bf16[2048,768]{1,0:T(8,128)(2,1)}) %all-gather.9.cloned.1.call-update) | async-done | bytes 3145744 | tf_op jit(solution)/shard_map/while/body/eval_jaxpr/all_gather | solution.py:201
  1642.0 31.6 %multiply_reduce_fusion.12 = (f32[12,512]{1,0:T(8,128)S(1)}, f32[12,512,2048]{2,1,0:T(8,128)}) fusion(f32[12,512,2048]{2,1,0:T(8,128)} %get-tuple-element.2142, f32[12,512]{1,0:T(8,128)S(1)} %get-tuple-element.2143, bf16[512,12,64]{0,2,1:T(8,128)(2,1)} %bitcast.291, bf16[2048,12,64]{0,2,1:T(8,128)(2,1)S(1)} %bitcast.281), kind=kOutput, calls=%fused_computation.105.clone.1 | convolution fusion | flops 1648355328 | bytes 104644608 | tf_op jit(solution)/shard_map/while/body/eval_jaxpr/qhe,khe->hqk/dot_general | solution.py:230
  1673.7 41.0 %multiply_convert_fusion.9 = bf16[12,512,2048]{2,1,0:T(8,128)(2,1)} fusion(f32[12,512,2048]{2,1,0:T(8,128)} %get-tuple-element.2153, f32[12,512]{1,0:T(8,128)S(1)} %get-tuple-element.2154, f32[12,512,2048]{2,1,0:T(8,128)} %get-tuple-element.2142, f32[12,512]{1,0:T(8,128)S(1)} %get-tuple-element.2143), kind=kLoop, calls=%fused_computation.104.clone.1 | loop fusion | flops 50331648 | bytes 125878272 | tf_op jit(solution)/shard_map/while/body/eval_jaxpr/convert_element_type | solution.py:234
  1767.8 27.4 %reduce-scatter.17.cloned.1.call-done = bf16[512,768]{0,1:T(8,128)(2,1)} async-done(((bf16[2048,768]{0,1:T(8,128)(2,1)}), bf16[512,768]{0,1:T(8,128)(2,1)}) %reduce-scatter.17.cloned.1.call-update) | async-done | bytes 786448 | tf_op jit(solution)/shard_map/while/body/eval_jaxpr/reduce_scatter | solution.py:258
  1830.9 60.4 %all-reduce.9 = (f32[768]{0:T(1024)S(1)}, f32[768]{0:T(1024)S(1)}, f32[768]{0:T(1024)S(1)}, f32[768]{0:T(1024)S(1)}, f32[768]{0:T(1024)S(1)}, /*index=5*/f32[768...) all-reduce(f32[768]{0:T(1024)S(1)} %copy-done.71, ...), channel_id=4, replica_groups=mesh['section'=2,'dp'=4,'seq'=4] {'dp','seq'}, use_global_device_ids=true, to_apply=%region_34.35.clone | all-reduce | flops 9216 | bytes 73728
  1896.6 90.9 %reduce-scatter.7.cloned.1.call-done = f32[48,2304]{1,0:T(8,128)} async-done(((f32[768,2304]{1,0:T(8,128)}), f32[48,2304]{1,0:T(8,128)}) %reduce-scatter.7.cloned.1.call-update) | async-done | bytes 442384 | tf_op jit(solution)/shard_map/reduce_scatter | solution.py:310
  1987.5 116.1 %reduce-scatter.13.cloned.1.call-done = f32[192,768]{1,0:T(8,128)} async-done(((f32[3072,768]{1,0:T(8,128)}), f32[192,768]{1,0:T(8,128)}) %reduce-scatter.13.cloned.1.call-update) | async-done | bytes 589840 | tf_op jit(solution)/shard_map/reduce_scatter | solution.py:310
  2103.6 117.0 %reduce-scatter.11.cloned.1.call-done = f32[48,3072]{1,0:T(8,128)} async-done(((f32[768,3072]{1,0:T(8,128)}), f32[48,3072]{1,0:T(8,128)}) %reduce-scatter.11.cloned.1.call-update) | async-done | bytes 589840 | tf_op jit(solution)/shard_map/reduce_scatter | solution.py:310
  (842 shorter events, 843.7 us)
Async XLA Ops:
  16.6 74.8 %all-gather.7.cloned.1.call-start = ((), (), s32[]{:S(2)}) async-start(), calls=%async_computation.11 | async-start | bytes 3932160 | tf_op jit(solution)/shard_map/while/body/eval_jaxpr/all_gather | solution.py:168
  25.0 130.1 %all-gather.5.cloned.1.call-start = ((), (), s32[]{:S(2)}) async-start(), calls=%async_computation.10 | async-start | bytes 3932160 | tf_op jit(solution)/shard_map/while/body/eval_jaxpr/all_gather | solution.py:169
  204.4 20.4 collective-permute-start
  224.8 71.8 %all-gather.7.cloned.1.call-start = ((), (), s32[]{:S(2)}) async-start(), calls=%async_computation.11 | async-start | bytes 3932160 | tf_op jit(solution)/shard_map/while/body/eval_jaxpr/all_gather | solution.py:168
  233.3 127.0 %all-gather.5.cloned.1.call-start = ((), (), s32[]{:S(2)}) async-start(), calls=%async_computation.10 | async-start | bytes 3932160 | tf_op jit(solution)/shard_map/while/body/eval_jaxpr/all_gather | solution.py:169
  409.5 20.4 collective-permute-start
  430.0 71.8 %all-gather.7.cloned.1.call-start = ((), (), s32[]{:S(2)}) async-start(), calls=%async_computation.11 | async-start | bytes 3932160 | tf_op jit(solution)/shard_map/while/body/eval_jaxpr/all_gather | solution.py:168
  438.4 127.0 %all-gather.5.cloned.1.call-start = ((), (), s32[]{:S(2)}) async-start(), calls=%async_computation.10 | async-start | bytes 3932160 | tf_op jit(solution)/shard_map/while/body/eval_jaxpr/all_gather | solution.py:169
  614.7 20.4 collective-permute-start
  637.4 162.0 %copy-start.30 = (f32[768]{0:T(1024)}, f32[768]{0:T(1024)S(1)}, u32[]{:S(2)}) copy-start(f32[768]{0:T(1024)S(1)} %get-tuple-element.2357) | copy-start | bytes 9220 | tf_op jit(solution)/shard_map/while
  637.4 188.5 %copy-start.28 = (f32[768]{0:T(1024)}, f32[768]{0:T(1024)S(1)}, u32[]{:S(2)}) copy-start(f32[768]{0:T(1024)S(1)} %get-tuple-element.2356) | copy-start | bytes 9220 | tf_op jit(solution)/shard_map/while
  637.4 71.4 %all-gather.11.cloned.1.call-start = ((), (), s32[]{:S(2)}) async-start(), calls=%async_computation.13 | async-start | bytes 3932160 | tf_op jit(solution)/shard_map/while/body/eval_jaxpr/all_gather | solution.py:200
  645.4 127.1 %all-gather.9.cloned.1.call-start = ((), (), s32[]{:S(2)}) async-start(), calls=%async_computation.12 | async-start | bytes 3932160 | tf_op jit(solution)/shard_map/while/body/eval_jaxpr/all_gather | solution.py:201
  648.5 322.7 %reduce-scatter.15.cloned.1.call-start = ((), (), s32[]{:S(2)}) async-start(), calls=%async_computation.14 | async-start | bytes 3932160 | tf_op jit(solution)/shard_map/while/body/eval_jaxpr/reduce_scatter | solution.py:261
  882.4 121.5 %reduce-scatter.17.cloned.1.call-start = ((), (), s32[]{:S(2)}) async-start(), calls=%async_computation.15 | async-start | bytes 3932160 | tf_op jit(solution)/shard_map/while/body/eval_jaxpr/reduce_scatter | solution.py:258
  1012.1 21.0 collective-permute-start.1
  1033.4 188.2 %copy-start.28 = (f32[768]{0:T(1024)}, f32[768]{0:T(1024)S(1)}, u32[]{:S(2)}) copy-start(f32[768]{0:T(1024)S(1)} %get-tuple-element.2356) | copy-start | bytes 9220 | tf_op jit(solution)/shard_map/while
  1033.4 71.0 %all-gather.11.cloned.1.call-start = ((), (), s32[]{:S(2)}) async-start(), calls=%async_computation.13 | async-start | bytes 3932160 | tf_op jit(solution)/shard_map/while/body/eval_jaxpr/all_gather | solution.py:200
  1041.4 126.6 %all-gather.9.cloned.1.call-start = ((), (), s32[]{:S(2)}) async-start(), calls=%async_computation.12 | async-start | bytes 3932160 | tf_op jit(solution)/shard_map/while/body/eval_jaxpr/all_gather | solution.py:201
  1044.5 327.7 %reduce-scatter.15.cloned.1.call-start = ((), (), s32[]{:S(2)}) async-start(), calls=%async_computation.14 | async-start | bytes 3932160 | tf_op jit(solution)/shard_map/while/body/eval_jaxpr/reduce_scatter | solution.py:261
  1278.1 121.5 %reduce-scatter.17.cloned.1.call-start = ((), (), s32[]{:S(2)}) async-start(), calls=%async_computation.15 | async-start | bytes 3932160 | tf_op jit(solution)/shard_map/while/body/eval_jaxpr/reduce_scatter | solution.py:258
  1407.9 21.0 collective-permute-start.1
  1429.2 187.9 %copy-start.28 = (f32[768]{0:T(1024)}, f32[768]{0:T(1024)S(1)}, u32[]{:S(2)}) copy-start(f32[768]{0:T(1024)S(1)} %get-tuple-element.2356) | copy-start | bytes 9220 | tf_op jit(solution)/shard_map/while
  1429.2 71.0 %all-gather.11.cloned.1.call-start = ((), (), s32[]{:S(2)}) async-start(), calls=%async_computation.13 | async-start | bytes 3932160 | tf_op jit(solution)/shard_map/while/body/eval_jaxpr/all_gather | solution.py:200
  1437.2 126.6 %all-gather.9.cloned.1.call-start = ((), (), s32[]{:S(2)}) async-start(), calls=%async_computation.12 | async-start | bytes 3932160 | tf_op jit(solution)/shard_map/while/body/eval_jaxpr/all_gather | solution.py:201
  1440.3 327.5 %reduce-scatter.15.cloned.1.call-start = ((), (), s32[]{:S(2)}) async-start(), calls=%async_computation.14 | async-start | bytes 3932160 | tf_op jit(solution)/shard_map/while/body/eval_jaxpr/reduce_scatter | solution.py:261
  1673.6 121.5 %reduce-scatter.17.cloned.1.call-start = ((), (), s32[]{:S(2)}) async-start(), calls=%async_computation.15 | async-start | bytes 3932160 | tf_op jit(solution)/shard_map/while/body/eval_jaxpr/reduce_scatter | solution.py:258
  1803.4 21.0 collective-permute-start.1
  1826.4 70.2 %reduce-scatter.9.cloned.1.call-start = ((), (), s32[]{:S(2)}) async-start(), calls=%async_computation.7 | async-start | bytes 2506752 | tf_op jit(solution)/shard_map/reduce_scatter | solution.py:310
  1827.0 160.5 %reduce-scatter.7.cloned.1.call-start = ((), (), s32[]{:S(2)}) async-start(), calls=%async_computation.6 | async-start | bytes 7520256 | tf_op jit(solution)/shard_map/reduce_scatter | solution.py:310
  1827.6 276.0 %reduce-scatter.13.cloned.1.call-start = ((), (), s32[]{:S(2)}) async-start(), calls=%async_computation.9 | async-start | bytes 10027008 | tf_op jit(solution)/shard_map/reduce_scatter | solution.py:310
  1828.2 392.5 %reduce-scatter.11.cloned.1.call-start = ((), (), s32[]{:S(2)}) async-start(), calls=%async_computation.8 | async-start | bytes 10027008 | tf_op jit(solution)/shard_map/reduce_scatter | solution.py:310
  (255 other events, 3216.1 us)
Sparse Core Ops, SparseCore 0:
  25.1 66.1 all-gather.6
  92.9 62.1 all-gather.4
  233.4 63.1 all-gather.6
  298.1 62.1 all-gather.4
  438.5 63.2 all-gather.6
  503.2 62.1 all-gather.4
  645.5 63.2 all-gather.10
  710.3 62.1 all-gather.8
  882.5 58.8 reduce-scatter.14
  943.6 60.2 reduce-scatter.16
  1041.6 62.8 all-gather.10
  1105.8 62.1 all-gather.8
  1278.2 58.8 reduce-scatter.14
  1339.3 60.2 reduce-scatter.16
  1437.3 62.8 all-gather.10
  1501.6 62.1 all-gather.8
  1673.7 58.8 reduce-scatter.14
  1734.8 60.2 reduce-scatter.16
Sparse Core Ops, SparseCore 1:
  1831.2 62.3 reduce-scatter.8
  1898.5 88.9 reduce-scatter.6
  1992.0 111.5 reduce-scatter.12
  2108.9 111.7 reduce-scatter.10
where the time goes:
time: 2250 us; the launch traced here: 2230 us
  waiting for transfers between devices  1040 us (46%)
  matrix products  782 us (35%)
  other arithmetic  189 us (8%)
  local copies, waits for them, and re-layouts  113 us (5%)
  blocking collectives  60.4 us (3%)
    reduce_scatter x4, waiting for transfers between devices, on_device(): lax.psum_scatter(totals, ('dp', 'seq'), scatter_dimension=0, tiled=True)  324 us
    all_gather x3, waiting for transfers between devices, forward_tick(): lax.all_gather(keys_out, 'seq', axis=0, tiled=True)  174 us
    all_gather x3, waiting for transfers between devices, backward_tick(): lax.all_gather(keys_out, 'seq', axis=0, tiled=True)  163 us
    sub x6, matrix products, softmax_parts(): raised = jnp.exp(scores - highest[..., None])  147 us
    convert_element_type x3, other arithmetic, backward_tick(): (soft_probs * (d_probs - delta_rows[..., None])).astype(jnp.bfloat16)  123 us
    dot_general x6, matrix products, attend(): jnp.einsum('hqk,khe->qhe', low_probs, split_heads(values_all), preferred_...  117 us
    all_gather x3, waiting for transfers between devices, backward_tick(): lax.all_gather(values_out, 'seq', axis=0, tiled=True)  106 us
    all_gather x3, waiting for transfers between devices, forward_tick(): lax.all_gather(values_out, 'seq', axis=0, tiled=True)  105 us
  transfers between devices with their start and end apart: 28, of which 24 were waited for; matrix products, arithmetic and copies ran while one was open for 24% of the time, Pallas kernels for 0%

commit v1 on v0

--- a/solution.py
+++ b/solution.py
@@ -3,6 +3,8 @@
 import jax
 import jax.numpy as jnp
 from jax import lax
+from jax.experimental import pallas as pl
+from jax.experimental.pallas import tpu as pltpu
 from jax.sharding import PartitionSpec as P
 
 HEADS = 12
@@ -327,6 +329,1303 @@
     )
 
 
+HEAD = 64
+BIG = 1e30
+NT = (((1,), (1,)), ((), ()))
+F32 = jnp.float32
+BF16 = jnp.bfloat16
+BLK = 256
+CH = 256
+FINE = 128
+PIECE = 512
+UN = 8
+
+def lane_mask(shape, h):
+    lane = lax.broadcasted_iota(jnp.int32, shape, len(shape) - 1)
+    return (lane < HEAD) if h == 0 else (lane >= HEAD)
+
+def only(x, h):
+    return jnp.where(lane_mask(x.shape, h), x, jnp.zeros_like(x))
+
+def fwd_kernel(lo_ref, hi_ref, q_ref, k_ref, v_ref, fq_ref, fk_ref, o_ref, lse_ref):
+    i = pl.program_id(0)
+    n, w = k_ref.shape
+    pairs = w // 128
+    lo = lo_ref[i]
+    count = hi_ref[i] - lo
+
+    def run(lo, c):
+        fq = fq_ref[...]
+        at = pl.multiple_of(lo * FINE, FINE)
+        pieces = []
+        done = 0
+        while done < c * FINE:
+            size = min(PIECE, c * FINE - done)
+            pieces.append(pl.ds(pl.multiple_of(at + done, FINE), size))
+            done += size
+
+        def scores(u, rows):
+            p, h = divmod(u, 2)
+            cols = slice(p * 128, (p + 1) * 128)
+            q = q_ref[:, cols] * jnp.asarray(SCALE, BF16)
+            qa = jnp.concatenate([only(q, h), fq], axis=1)
+            kb = jnp.concatenate([k_ref[rows, cols], fk_ref[rows, :]], axis=1)
+            return lax.dot_general(qa, kb, NT, preferred_element_type=F32)
+
+        now = [scores(0, rows) for rows in pieces]
+        outs, lses = [], []
+        for u in range(2 * pairs):
+            p, h = divmod(u, 2)
+            cols = slice(p * 128, (p + 1) * 128)
+            m = jnp.max(now[0], axis=1, keepdims=True)
+            for s in now[1:]:
+                m = jnp.maximum(m, jnp.max(s, axis=1, keepdims=True))
+            r = None
+            later = []
+            for s, rows in zip(now, pieces):
+                if u + 1 < 2 * pairs:
+                    later.append(scores(u + 1, rows))
+                pr = jnp.exp(s - m).astype(BF16)
+                vb = jnp.concatenate([v_ref[rows, cols], jnp.ones((s.shape[1], 128), BF16)], axis=1)
+                part = jnp.dot(pr, vb, preferred_element_type=F32)
+                r = part if r is None else r + part
+            now = later
+            l = r[:, 128:]
+            outs.append(r[:, :128] / l)
+            lses.append(m + jnp.log(l))
+            if h == 1:
+                mask = lane_mask((BLK, 128), 0)
+                o_ref[:, cols] = jnp.where(mask, outs[0], outs[1]).astype(BF16)
+                both = jnp.where(mask, lses[0], lses[1]).T
+                lse_ref[p, 0:1, :] = both[0:1, :]
+                lse_ref[p, 1:2, :] = both[HEAD:HEAD + 1, :]
+                outs, lses = [], []
+
+    most = n // FINE
+    below = 0
+    for c in sorted({max(BLK // FINE, most * e // 16) for e in (2, 4, 6, 8, 11, 13, 14, 16)}):
+        @pl.when((count > below) & (count <= c))
+        def _(c=c):
+            run(jnp.minimum(lo, most - c), c)
+        below = c
+
+def attn_fwd(lo, hi, q, k, v, fq, fk):
+    n, w = q.shape
+    pairs = w // 128
+    blk = lambda i, lo, hi: (i, 0)
+    full = lambda i, lo, hi: (0, 0)
+    return pl.pallas_call(
+        fwd_kernel,
+        grid_spec=pltpu.PrefetchScalarGridSpec(
+            num_scalar_prefetch=2,
+            grid=(n // BLK,),
+            in_specs=[pl.BlockSpec((BLK, w), blk), pl.BlockSpec((n, w), full), pl.BlockSpec((n, w), full),
+                      pl.BlockSpec((BLK, 128), blk), pl.BlockSpec((n, 128), full)],
+            out_specs=[pl.BlockSpec((BLK, w), blk), pl.BlockSpec((pairs, 8, BLK), lambda i, lo, hi: (0, 0, i))],
+        ),
+        out_shape=[jax.ShapeDtypeStruct((n, w), BF16), jax.ShapeDtypeStruct((pairs, 8, n), F32)],
+        compiler_params=pltpu.CompilerParams(vmem_limit_bytes=62 * 2 ** 20),
+        name="attn_fwd",
+    )(lo, hi, q, k, v, fq, fk)
+
+def bwd_kernel(lo_ref, hi_ref, q_ref, k_ref, v_ref, do_ref, o_ref, lse_ref, fq_ref, fk_ref,
+               dq_ref, dk_ref, dv_ref, delta, dqt, dk_acc, dv_acc):
+    j = pl.program_id(0)
+    nb = pl.num_programs(0)
+    n, w = q_ref.shape
+    pairs = w // 128
+
+    @pl.when(j == 0)
+    def _():
+        head = lax.broadcasted_iota(jnp.int32, (16, 128), 0)
+        lane = lax.broadcasted_iota(jnp.int32, (16, 128), 1)
+        sel = jnp.where(lane // HEAD == head, 1.0, 0.0).astype(BF16)
+
+        def prep(b, c):
+            rows = pl.ds(pl.multiple_of(b * CH, CH), CH)
+            for p in range(pairs):
+                cols = slice(p * 128, (p + 1) * 128)
+                prod = do_ref[rows, cols].astype(F32) * o_ref[rows, cols].astype(F32)
+                hi = prod.astype(BF16)
+                lo = (prod - hi.astype(F32)).astype(BF16)
+                d = lax.dot_general(sel, hi, NT, preferred_element_type=F32) + lax.dot_general(sel, lo, NT, preferred_element_type=F32)
+                delta[p, :, rows] = d[0:8, :]
+                dqt[p, :, rows] = jnp.zeros((128, CH), F32)
+            return c
+        lax.fori_loop(0, n // CH, prep, 0)
+
+    lo = lo_ref[j]
+    count = hi_ref[j] - lo
+    dk_acc[...] = jnp.zeros_like(dk_acc)
+    dv_acc[...] = jnp.zeros_like(dv_acc)
+
+    def run(first, c):
+        rows = pl.ds(pl.multiple_of(first * FINE, FINE), c * FINE)
+        units = 2 * pairs
+
+        def scores(u):
+            p, h = divmod(u, 2)
+            cols = slice(p * 128, (p + 1) * 128)
+            kb = jnp.concatenate([only(k_ref[:, cols] * jnp.asarray(SCALE, BF16), h), fk_ref[...]], axis=1)
+            qa = jnp.concatenate([q_ref[rows, cols], fq_ref[rows, :]], axis=1)
+            s = lax.dot_general(kb, qa, NT, preferred_element_type=F32)
+            dp = lax.dot_general(only(v_ref[:, cols], h), do_ref[rows, cols], NT, preferred_element_type=F32)
+            return s, dp
+
+        now = scores(0)
+        dk, dv = [], []
+        for u in range(units):
+            p, h = divmod(u, 2)
+            cols = slice(p * 128, (p + 1) * 128)
+            later = scores(u + 1) if u + 1 < units else None
+            s, dp = now
+            pr = jnp.exp(s - lse_ref[p, h:h + 1, rows])
+            ds = (pr * (dp - delta[p, h:h + 1, rows])).astype(BF16)
+            dv.append(jnp.dot(pr.astype(BF16), do_ref[rows, cols], preferred_element_type=F32))
+            dk.append(jnp.dot(ds, q_ref[rows, cols], preferred_element_type=F32))
+            kt = (k_ref[:, cols] * jnp.asarray(SCALE, BF16)).T
+            dqt[p, h * HEAD:(h + 1) * HEAD, rows] += jnp.dot(kt[h * HEAD:(h + 1) * HEAD, :], ds, preferred_element_type=F32)
+            now = later
+            if h == 1:
+                mask = lane_mask((BLK, 128), 0)
+                dk_acc[:, cols] += jnp.where(mask, dk[0], dk[1])
+                dv_acc[:, cols] += jnp.where(mask, dv[0], dv[1])
+                dk, dv = [], []
+
+    @pl.loop(0, count // UN)
+    def _(t):
+        run(lo + t * UN, UN)
+
+    left = count % UN
+    for c in range(1, UN):
+        @pl.when(left == c)
+        def _(c=c):
+            run(lo + (count - left), c)
+    dk_ref[...] = (dk_acc[...] * SCALE).astype(BF16)
+    dv_ref[...] = dv_acc[...].astype(BF16)
+
+    @pl.when(j == nb - 1)
+    def _():
+        def fin(b, c):
+            rows = pl.ds(pl.multiple_of(b * CH, CH), CH)
+            for p in range(pairs):
+                dq_ref[rows, p * 128:(p + 1) * 128] = dqt[p, :, rows].T.astype(BF16)
+            return c
+        lax.fori_loop(0, n // CH, fin, 0)
+
+def attn_bwd(lo, hi, q, k, v, do, o, lse, fq, fk):
+    n, w = q.shape
+    pairs = w // 128
+    full = lambda j, lo, hi: (0, 0)
+    blk = lambda j, lo, hi: (j, 0)
+    sh = jax.ShapeDtypeStruct((n, w), BF16)
+    big = pl.BlockSpec((n, w), full, pipeline_mode=pl.Buffered(1))
+    return pl.pallas_call(
+        bwd_kernel,
+        grid_spec=pltpu.PrefetchScalarGridSpec(
+            num_scalar_prefetch=2,
+            grid=(n // BLK,),
+            in_specs=[big, pl.BlockSpec((BLK, w), blk), pl.BlockSpec((BLK, w), blk), big, big, pl.BlockSpec((pairs, 8, n), lambda j, lo, hi: (0, 0, 0)),
+                      pl.BlockSpec((n, 128), full), pl.BlockSpec((BLK, 128), blk)],
+            out_specs=[pl.BlockSpec((n, w), full), pl.BlockSpec((BLK, w), blk), pl.BlockSpec((BLK, w), blk)],
+            scratch_shapes=[
+                pltpu.VMEM((pairs, 8, n), F32),
+                pltpu.VMEM((pairs, 128, n), F32),
+                pltpu.VMEM((BLK, w), F32),
+                pltpu.VMEM((BLK, w), F32),
+            ],
+        ),
+        out_shape=[sh, sh, sh],
+        compiler_params=pltpu.CompilerParams(vmem_limit_bytes=62 * 2 ** 20),
+        name="attn_bwd",
+    )(lo, hi, q, k, v, do, o, lse, fq, fk)
+
+def segment_terms(lengths, n):
+    cells = lengths.shape[0]
+    place_of = jnp.arange(cells)
+    ends = jnp.sum(jnp.where(place_of[:, None] <= place_of[None, :], lengths[:, None], 0), axis=0)
+    starts = ends - lengths
+    pos = jnp.arange(n, dtype=jnp.int32)[:, None]
+    pad = lambda v: jnp.pad(v, (0, 128 - cells))[None, :]
+    hot = (pos >= pad(starts)) & (pos < pad(ends))
+    used = (jnp.arange(128) < cells)[None, :]
+    fq = jnp.where(hot, -BIG, 0.0).astype(BF16)
+    fk = jnp.where(used & ~hot, 1.0, 0.0).astype(BF16)
+    first = jnp.arange(n // BLK, dtype=jnp.int32)[:, None] * BLK
+    lo = jnp.max(jnp.where(starts[None, :] <= first, starts[None, :], 0), axis=1) // FINE
+    hi = (jnp.min(jnp.where(ends[None, :] > first + BLK - 1, ends[None, :], n), axis=1) + FINE - 1) // FINE
+    return fq, fk, lo.astype(jnp.int32), hi.astype(jnp.int32)
+
+
+MIB = 2 ** 20
+MESH = pl.DeviceIdType.MESH
+ANY = pl.BlockSpec(memory_space=pl.ANY)
+VMEM = pl.BlockSpec(memory_space=pltpu.VMEM)
+DMA = pltpu.SemaphoreType.DMA
+TOK = 256
+COLS = 768
+
+
+def sds(shape, dtype):
+    return jax.ShapeDtypeStruct(shape, dtype)
+
+
+def place():
+    section, dp, seq = lax.axis_index("section"), lax.axis_index("dp"), lax.axis_index("seq")
+    core = lax.rem(dp, 2)
+    return section, dp, seq, core
+
+
+def greet(*devices):
+    barrier = pltpu.get_barrier_semaphore()
+    for device in devices:
+        pl.semaphore_signal(barrier, 1, device_id=device, device_id_type=MESH)
+    pl.semaphore_wait(barrier, len(devices))
+
+
+def column_mates(section, dp, seq, core):
+    mates = [(section, dp, lax.rem(seq + t, 4)) for t in range(1, 4)]
+    mates += [(section, dp + 1 - 2 * core, lax.rem(seq + t, 4)) for t in range(4)]
+    return mates
+
+
+def remote(src, dst, send_sem, recv_sem, device):
+    return pltpu.make_async_remote_copy(
+        src_ref=src, dst_ref=dst, send_sem=send_sem, recv_sem=recv_sem,
+        device_id=device, device_id_type=MESH,
+    )
+
+
+def span(start, size):
+    return pl.ds(pl.multiple_of(start, size), size)
+
+
+def chunk(i):
+    return span(i * TOK, TOK)
+
+
+def row_norm(values):
+    centre = jnp.mean(values, axis=-1, keepdims=True)
+    offset = values - centre
+    spread = jnp.mean(offset * offset, axis=-1, keepdims=True)
+    rstd = lax.rsqrt(spread + EPS)
+    return offset * rstd, rstd
+
+
+def row_norm_back(grad, hat, rstd, gain):
+    d_hat = grad * gain
+    mean_d = jnp.mean(d_hat, axis=-1, keepdims=True)
+    mean_dh = jnp.mean(d_hat * hat, axis=-1, keepdims=True)
+    return rstd * (d_hat - mean_d - hat * mean_dh)
+
+
+def fold(values):
+    return jnp.sum(values.reshape(values.shape[0] // 8, 8, values.shape[1]), axis=0)
+
+
+def up(ref):
+    return ref[...].astype(F32)
+
+
+def gelu_parts(x):
+    size = jnp.abs(x)
+    d = 1.0 + 0.2316418882 * size
+    t = pl.reciprocal(d, approx=True)
+    t = t * (2.0 - d * t)
+    density = jnp.exp(-0.5 * (x * x)) * 0.3989422804014327
+    poly = ((((1.330274429 * t - 1.821255978) * t + 1.781477937) * t - 0.356563782) * t + 0.319381530) * t
+    tail = density * poly
+    phi = jnp.where(x >= 0.0, 1.0 - tail, tail)
+    return x * phi, phi + x * density
+
+
+def ffn_loads(wo_in, win_in, wback_in, wo, win, wback, sem):
+    pairs = [(wo_in, wo)]
+    for f in range(win.shape[1] // COLS):
+        cols = pl.ds(f * COLS, COLS)
+        pairs += [(win_in.at[:, cols], win.at[:, cols]), (wback_in.at[cols], wback.at[cols])]
+    return [pltpu.make_async_copy(a, b, sem.at[n]) for n, (a, b) in enumerate(pairs)]
+
+
+class ToHeads:
+    def __init__(self, buf, outs, tokens, width, sems, core, sibling):
+        self.buf, self.outs, self.tokens, self.width = buf, outs, tokens, width
+        self.own_sem, self.send_sem, self.recv_sem = sems
+        self.core, self.sibling = core, sibling
+
+    def _cols(self, part, core):
+        return span(part * self.width + core * (self.width // 2), self.width // 2)
+
+    def _sent(self, i, part, owner):
+        rows = span(owner * self.tokens + i * TOK, TOK)
+        return remote(self.buf.at[chunk(i), self._cols(part, 1 - self.core)], self.outs[part].at[rows],
+                      self.send_sem.at[part, i], self.recv_sem.at[part, i], self.sibling)
+
+    def _own(self, i, part):
+        rows = span(self.core * self.tokens + i * TOK, TOK)
+        return pltpu.make_async_copy(self.buf.at[chunk(i), self._cols(part, self.core)],
+                                     self.outs[part].at[rows], self.own_sem.at[part, i])
+
+    def start(self, i):
+        for part in range(len(self.outs)):
+            self._own(i, part).start()
+            self._sent(i, part, self.core).start()
+
+    def wait(self, i):
+        for part in range(len(self.outs)):
+            self._own(i, part).wait()
+            self._sent(i, part, self.core).wait_send()
+            self._sent(i, part, 1 - self.core).wait_recv()
+
+
+class ToTokens:
+    def __init__(self, ins, buf, tokens, width, sems, core, sibling):
+        self.ins, self.buf, self.tokens, self.width = ins, buf, tokens, width
+        self.own_sem, self.send_sem, self.recv_sem = sems
+        self.core, self.sibling = core, sibling
+
+    def _cols(self, part, core):
+        return span(part * self.width + core * (self.width // 2), self.width // 2)
+
+    def _sent(self, i, part, owner):
+        rows = span((1 - self.core) * self.tokens + i * TOK, TOK)
+        return remote(self.ins[part].at[rows], self.buf.at[chunk(i), self._cols(part, owner)],
+                      self.send_sem.at[part, i], self.recv_sem.at[part, i], self.sibling)
+
+    def _own(self, i, part):
+        rows = span(self.core * self.tokens + i * TOK, TOK)
+        return pltpu.make_async_copy(self.ins[part].at[rows], self.buf.at[chunk(i), self._cols(part, self.core)],
+                                     self.own_sem.at[part, i])
+
+    def start(self, i):
+        for part in range(len(self.ins)):
+            self._own(i, part).start()
+            self._sent(i, part, self.core).start()
+
+    def wait(self, i):
+        for part in range(len(self.ins)):
+            self._own(i, part).wait()
+            self._sent(i, part, 1 - self.core).wait_recv()
+
+    def wait_sent(self, i):
+        for part in range(len(self.ins)):
+            self._sent(i, part, self.core).wait_send()
+
+
+def swap_sems(parts, steps):
+    return [DMA((parts, steps))] * 3
+
+
+class Blocks:
+    def __init__(self, rows_ref, blocks_ref, gather, sems, section, dp, seq, core):
+        self.rows, self.blocks, self.gather = rows_ref, blocks_ref, gather
+        self.own_sem, self.send_sem, self.recv_sem = sems
+        self.section, self.seq, self.core, self.column = section, seq, core, dp - core
+        self.each, self.local, _ = blocks_ref.shape
+
+    def _move(self, j):
+        target_core, target_seq = self.seq // self.each, self.core * self.each + j
+        slot = lax.rem(self.seq, self.each)
+        here = (target_core == self.core) & (target_seq == self.seq)
+        if self.gather:
+            src, dst = self.blocks.at[j], self.rows.at[span(slot * self.local, self.local)]
+        else:
+            src, dst = self.rows.at[pl.ds(j * self.local, self.local)], self.blocks.at[slot]
+        target = (self.section, self.column + target_core, target_seq)
+        return here, src, dst, slot, target
+
+    def start(self):
+        for j in range(self.each):
+            here, src, dst, slot, target = self._move(j)
+
+            @pl.when(here)
+            def _():
+                pltpu.make_async_copy(src, dst, self.own_sem).start()
+
+            @pl.when(jnp.logical_not(here))
+            def _():
+                remote(src, dst, self.send_sem.at[j], self.recv_sem.at[slot], target).start()
+
+    def wait(self):
+        for j in range(self.each):
+            here, src, dst, slot, target = self._move(j)
+
+            @pl.when(here)
+            def _():
+                pltpu.make_async_copy(src, dst, self.own_sem).wait()
+
+            @pl.when(jnp.logical_not(here))
+            def _():
+                remote(src, dst, self.send_sem.at[j], self.recv_sem.at[slot], target).wait_send()
+        for j in range(self.each):
+            here = (self.seq // self.each == self.core) & (self.core * self.each + j == self.seq)
+            mate = (self.section, self.column + 1 - self.core, self.seq)
+            if self.gather:
+                dst = self.rows.at[pl.ds(j * self.local, self.local)]
+                src = self.blocks.at[0]
+            else:
+                dst = self.blocks.at[j]
+                src = self.rows.at[pl.ds(0, self.local)]
+
+            @pl.when(jnp.logical_not(here))
+            def _():
+                remote(src, dst, self.send_sem.at[0], self.recv_sem.at[j], mate).wait_recv()
+
+
+def block_sems(each):
+    return [DMA, DMA((each,)), DMA((each,))]
+
+
+def project(x, gain, bias, w, qb, vb, buf, rows):
+    width = x.shape[1]
+    hat, _ = row_norm(x)
+    a = (hat * up(gain) + up(bias)).astype(BF16)
+    for part in range(3):
+        cols = slice(part * width, (part + 1) * width)
+        m = jnp.dot(a, w[:, cols], preferred_element_type=F32)
+        if part == 0:
+            m = m + up(qb)
+        if part == 2:
+            m = m + up(vb)
+        buf[rows, cols] = m.astype(BF16)
+    return a
+
+
+def first_kernel(x_ref, w_in, gain, bias, qb, vb, x_out, q_ref, k_ref, v_ref,
+                 xb, w, buf, w_sem, out_sem, own_sem, send_sem, recv_sem, *sems):
+    section, dp, seq, core = place()
+    sibling = (section, dp + 1 - 2 * core, seq)
+    each, local, width = x_ref.shape
+    part = local // 2
+    column = dp - core
+    load = pltpu.make_async_copy(w_in, w, w_sem)
+    load.start()
+    greet(*[(s, column + c, z) for s in range(2) for c in range(2) for z in range(2 * each)])
+
+    def move(m):
+        target_core, target_seq = seq // each, core * each + m
+        slot = lax.rem(seq, each)
+        here = (section == 0) & (target_core == core) & (target_seq == seq)
+        src = x_ref.at[m, span(section * part, part)]
+        dst = xb.at[span(slot * local + section * part, part)]
+        return here, src, dst, slot, (0, column + target_core, target_seq)
+
+    for m in range(each):
+        here, src, dst, slot, target = move(m)
+
+        @pl.when(here)
+        def _():
+            pltpu.make_async_copy(src, dst, own_sem).start()
+
+        @pl.when(jnp.logical_not(here))
+        def _():
+            remote(src, dst, send_sem.at[m], recv_sem.at[section, slot], target).start()
+    load.wait()
+
+    @pl.when(section == 0)
+    def _():
+        swap = ToHeads(buf, (q_ref, k_ref, v_ref), each * local, width, sems, core, sibling)
+
+        def out(i):
+            return pltpu.make_async_copy(xb.at[chunk(i)], x_out.at[chunk(i)], out_sem.at[i])
+
+        for h in range(2):
+            for j in range(each):
+                here = (seq // each == core) & (core * each + j == seq) & (h == 0)
+                dst = xb.at[pl.ds(j * local + h * part, part)]
+
+                @pl.when(here)
+                def _():
+                    pltpu.make_async_copy(x_ref.at[0, pl.ds(0, part)], dst, own_sem).wait()
+
+                @pl.when(jnp.logical_not(here))
+                def _():
+                    remote(x_ref.at[0, pl.ds(0, part)], dst, send_sem.at[0], recv_sem.at[h, j], sibling).wait_recv()
+
+                for i in range((j * local + h * part) // TOK, (j * local + (h + 1) * part) // TOK):
+                    rows = slice(i * TOK, (i + 1) * TOK)
+                    project(xb[rows, :].astype(F32), gain, bias, w, qb, vb, buf, rows)
+                    out(i).start()
+                    swap.start(i)
+        for i in range(each * local // TOK):
+            out(i).wait()
+            swap.wait(i)
+
+    for m in range(each):
+        here, src, dst, slot, target = move(m)
+
+        @pl.when(jnp.logical_not(here))
+        def _():
+            remote(src, dst, send_sem.at[m], recv_sem.at[section, slot], target).wait_send()
+
+
+def first_call(x, w, gain, bias, qb, vb):
+    each, local, width = x.shape
+    tokens = each * local
+    steps = tokens // TOK
+    out = sds((2 * tokens, width // 2), BF16)
+    return pl.pallas_call(
+        first_kernel,
+        in_specs=[ANY, ANY] + [VMEM] * 4,
+        out_specs=[ANY] * 4,
+        out_shape=[sds((tokens, width), BF16), out, out, out],
+        scratch_shapes=[
+            pltpu.VMEM((tokens, width), BF16), pltpu.VMEM(w.shape, BF16), pltpu.VMEM((tokens, 3 * width), BF16),
+            DMA, DMA((steps,)), DMA, DMA((each,)), DMA((2, each))] + swap_sems(3, steps),
+        compiler_params=pltpu.CompilerParams(collective_id=1, has_side_effects=True, vmem_limit_bytes=62 * MIB),
+        name="rows_qkv",
+    )(x, w, gain, bias, qb, vb)
+
+
+def feed(i, att, x, wo, win, wback, bo, g2, b2, bi, bb, keep=None, ready=None):
+    rows = chunk(i)
+    hidden = win.shape[1]
+    if ready:
+        ready[0].wait()
+    resid = x[rows, :].astype(F32) + up(bo) + jnp.dot(att[rows, :], wo[...], preferred_element_type=F32)
+    hat, rstd = row_norm(resid)
+    c = (hat * up(g2) + up(b2)).astype(BF16)
+    if keep is not None:
+        resid_b, slope_b, att_t, c_t, act_t = keep
+        resid_b[rows, :] = resid
+        att_t[:, rows] = att[rows, :].T
+        c_t[:, rows] = c.T
+    total = resid + up(bb)
+    for f in range(hidden // COLS):
+        cols = slice(f * COLS, (f + 1) * COLS)
+        if ready:
+            ready[1 + 2 * f].wait()
+            ready[2 + 2 * f].wait()
+        inner = jnp.dot(c, win[:, cols], preferred_element_type=F32) + bi[:, cols].astype(F32)
+        active, slope = gelu_parts(inner)
+        active = active.astype(BF16)
+        if keep is not None:
+            slope_b[rows, cols] = slope.astype(BF16)
+            act_t[cols, rows] = active.T
+        total = total + jnp.dot(active, wback[cols, :], preferred_element_type=F32)
+    return total
+
+
+def feed_back(i, dy, slope_b, resid_b, wo, win, wback, g2, di_b, dr_b, dp_b, da_b, sums):
+    rows = chunk(i)
+    hidden = win.shape[1]
+    g = dy.astype(F32)
+    d_c = jnp.zeros(dy.shape, F32)
+    for f in range(hidden // COLS):
+        cols = slice(f * COLS, (f + 1) * COLS)
+        d_active = lax.dot_general(dy, wback[cols, :], NT, preferred_element_type=F32)
+        d_inner = d_active * slope_b[rows, cols].astype(F32)
+        if sums:
+            sums[3][:, cols] += fold(d_inner)
+        d_inner = d_inner.astype(BF16)
+        if di_b is not None:
+            di_b[rows, cols] = d_inner
+        d_c = d_c + lax.dot_general(d_inner, win[:, cols], NT, preferred_element_type=F32)
+    hat, rstd = row_norm(resid_b[rows, :])
+    d_resid = g + row_norm_back(d_c, hat, rstd, up(g2))
+    d_proj = d_resid.astype(BF16)
+    dr_b[rows, :] = d_resid
+    if sums:
+        s_gain, s_bias, s_out, _, s_back = sums
+        s_gain[...] += fold(d_c * hat)
+        s_bias[...] += fold(d_c)
+        s_out[...] += fold(d_resid)
+        s_back[...] += fold(g)
+    if dp_b is not None:
+        dp_b[rows, :] = d_proj
+    da_b[rows, :] = lax.dot_general(d_proj, wo[...], NT, preferred_element_type=F32).astype(BF16)
+
+
+def pass_kernel(o_ref, x_ref, g_ref, wo_in, win_in, wback_in, wqkv_in, bo, g2, b2, bi, bb, g1, b1, qb, vb,
+                x_out, g_out, n_out, q_ref, k_ref, v_ref,
+                wo, win, wback, wqkv, att, yb, xn, buf, w_sem, x_send, x_recv, x_sem, *sems):
+    section, dp, seq, core = place()
+    sibling = (section, dp + 1 - 2 * core, seq)
+    across = (1 - section, dp, seq)
+    tokens, width = x_ref.shape
+    steps = tokens // TOK
+    loads = ffn_loads(wo_in, win_in, wback_in, wo, win, wback, w_sem)
+    load_qkv = pltpu.make_async_copy(wqkv_in, wqkv, w_sem.at[len(loads)])
+    loads[0].start()
+    greet(across, *column_mates(section, dp, seq, core))
+    to_tokens = ToTokens((o_ref,), att, tokens, width, sems[:3], core, sibling)
+    to_heads = ToHeads(buf, (q_ref, k_ref, v_ref), tokens, width, sems[3:6], core, sibling)
+    blocks = Blocks(g_out, g_ref, True, sems[6:9], section, dp, seq, core)
+    to_tokens.start(0)
+    for load in loads[1:]:
+        load.start()
+
+    @pl.loop(1, steps)
+    def _(i):
+        to_tokens.start(i)
+
+    load_qkv.start()
+
+    @pl.when(section == 1)
+    def _():
+        blocks.start()
+
+    def passed(i):
+        return remote(yb.at[chunk(i)], xn.at[chunk(i)], x_send.at[i], x_recv.at[i], across)
+
+    def kept(i):
+        return pltpu.make_async_copy(xn.at[chunk(i)], x_out.at[chunk(i)], x_sem.at[i])
+
+    def send_chunk(i, ready=None):
+        total = feed(i, att, x_ref, wo, win, wback, bo, g2, b2, bi, bb, ready=ready)
+        yb[chunk(i), :] = total.astype(BF16)
+        passed(i).start()
+        xn[chunk(i), :] = x_ref[chunk(i), :]
+
+    to_tokens.wait(0)
+
+    @pl.when(section == 0)
+    def _():
+        send_chunk(0, loads)
+
+    @pl.when(section == 1)
+    def _():
+        for load in loads:
+            load.wait()
+
+    @pl.loop(1, steps)
+    def _(i):
+        to_tokens.wait(i)
+
+        @pl.when(section == 0)
+        def _():
+            send_chunk(i)
+
+    load_qkv.wait()
+
+    @pl.loop(0, steps)
+    def _(i):
+        @pl.when(section == 1)
+        def _():
+            passed(i).wait_recv()
+
+        kept(i).start()
+        a = project(xn[chunk(i), :].astype(F32), g1, b1, wqkv, qb, vb, buf, chunk(i))
+        n_out[:, chunk(i)] = a.T
+        to_heads.start(i)
+
+    @pl.loop(0, steps)
+    def _(i):
+        to_tokens.wait_sent(i)
+        to_heads.wait(i)
+        kept(i).wait()
+
+        @pl.when(section == 0)
+        def _():
+            passed(i).wait_send()
+
+    @pl.when(section == 1)
+    def _():
+        blocks.wait()
+
+
+def pass_call(o, x, g, wo, win, wback, wqkv, vectors):
+    tokens, width = x.shape
+    steps = tokens // TOK
+    each = g.shape[0]
+    out = sds((2 * tokens, width // 2), BF16)
+    low = sds(x.shape, BF16)
+    low_buf = pltpu.VMEM(x.shape, BF16)
+    return pl.pallas_call(
+        pass_kernel,
+        in_specs=[ANY, VMEM, ANY, ANY, ANY, ANY, ANY] + [VMEM] * len(vectors),
+        out_specs=[ANY, ANY, VMEM, ANY, ANY, ANY],
+        out_shape=[low, low, sds((width, tokens), BF16), out, out, out],
+        scratch_shapes=[pltpu.VMEM(w.shape, BF16) for w in (wo, win, wback, wqkv)]
+        + [low_buf, low_buf, low_buf, pltpu.VMEM((tokens, 3 * width), BF16),
+           DMA((2 + 2 * (win.shape[1] // COLS),)), DMA((steps,)), DMA((steps,)), DMA((steps,))]
+        + swap_sems(1, steps) + swap_sems(3, steps) + block_sems(each),
+        compiler_params=pltpu.CompilerParams(collective_id=2, has_side_effects=True, vmem_limit_bytes=62 * MIB),
+        name="ffn_pass_qkv",
+    )(o, x, g, wo, win, wback, wqkv, *vectors)
+
+
+def turn_kernel(o_ref, x_ref, g_ref, wo_in, win_in, wback_in, bo, g2, b2, bi, bb,
+                y_out, resid_out, slope_out, att_out, c_out, act_out, dr_out, da_ref,
+                wo, win, wback, att, yb, resid_b, slope_b, att_t, c_t, act_t, dr_b, da_b,
+                w_sem, out_sem, *sems):
+    section, dp, seq, core = place()
+    sibling = (section, dp + 1 - 2 * core, seq)
+    tokens, width = x_ref.shape
+    steps = tokens // TOK
+    loads = ffn_loads(wo_in, win_in, wback_in, wo, win, wback, w_sem)
+    loads[0].start()
+    greet(sibling)
+    to_tokens = ToTokens((o_ref,), att, tokens, width, sems[:3], core, sibling)
+    to_heads = ToHeads(da_b, (da_ref,), tokens, width, sems[3:6], core, sibling)
+    to_tokens.start(0)
+    for load in loads[1:]:
+        load.start()
+
+    @pl.loop(1, steps)
+    def _(i):
+        to_tokens.start(i)
+
+    def results(i):
+        here = [(yb, y_out), (resid_b, resid_out), (slope_b, slope_out), (dr_b, dr_out)]
+        turned = [(att_t, att_out), (c_t, c_out), (act_t, act_out)]
+        return [pltpu.make_async_copy(b.at[chunk(i)], o.at[chunk(i)], out_sem.at[n, i])
+                for n, (b, o) in enumerate(here)] + [
+            pltpu.make_async_copy(b.at[:, chunk(i)], o.at[:, chunk(i)], out_sem.at[4 + n, i])
+            for n, (b, o) in enumerate(turned)]
+
+    def step(i, ready=None):
+        to_tokens.wait(i)
+        total = feed(i, att, x_ref, wo, win, wback, bo, g2, b2, bi, bb, (resid_b, slope_b, att_t, c_t, act_t), ready)
+        yb[chunk(i), :] = total.astype(BF16)
+        feed_back(i, g_ref[chunk(i), :], slope_b, resid_b, wo, win, wback, g2, None, dr_b, None, da_b, None)
+        to_heads.start(i)
+        for copy in results(i):
+            copy.start()
+
+    step(0, loads)
+
+    @pl.loop(1, steps)
+    def _(i):
+        step(i)
+
+    @pl.loop(0, steps)
+    def _(i):
+        to_tokens.wait_sent(i)
+        to_heads.wait(i)
+        for copy in results(i):
+            copy.wait()
+
+
+def turn_call(o, x, g, wo, win, wback, vectors):
+    tokens, width = x.shape
+    hidden = win.shape[1]
+    steps = tokens // TOK
+    low, full = sds(x.shape, BF16), sds(x.shape, F32)
+    turned = sds((width, tokens), BF16)
+    outs = [low, full, sds((tokens, hidden), BF16), turned, turned, sds((hidden, tokens), BF16), full]
+    buf = lambda s: pltpu.VMEM(s.shape, s.dtype)
+    return pl.pallas_call(
+        turn_kernel,
+        in_specs=[ANY, VMEM, VMEM, ANY, ANY, ANY] + [VMEM] * len(vectors),
+        out_specs=[ANY] * 8,
+        out_shape=outs + [sds((2 * tokens, width // 2), BF16)],
+        scratch_shapes=[buf(wo), buf(win), buf(wback), buf(low)] + [buf(s) for s in outs] + [buf(low)]
+        + [DMA((1 + 2 * (hidden // COLS),)), DMA((7, steps))] + swap_sems(1, steps) + swap_sems(1, steps),
+        compiler_params=pltpu.CompilerParams(collective_id=3, has_side_effects=True, vmem_limit_bytes=62 * MIB),
+        name="ffn_turn",
+    )(o, x, g, wo, win, wback, *vectors)
+
+
+def input_back(i, dj, dr, x, w, gain, sums):
+    rows = chunk(i)
+    width = x.shape[1]
+    d_a = lax.dot_general(dj[rows, :], w[...], NT, preferred_element_type=F32)
+    hat, rstd = row_norm(x[rows, :].astype(F32))
+    if sums:
+        s_gain, s_bias, s_q, s_v = sums
+        s_q[...] += fold(dj[rows, :width].astype(F32))
+        s_v[...] += fold(dj[rows, 2 * width:].astype(F32))
+        s_gain[...] += fold(d_a * hat)
+        s_bias[...] += fold(d_a)
+    return (dr[rows, :] + row_norm_back(d_a, hat, rstd, up(gain))).astype(BF16)
+
+
+def back_kernel(dq_ref, dk_ref, dv_ref, dr_ref, x_ref, y_ref, g_in, slope_in, resid_in,
+                wqkv_in, wo_in, win_in, wback_in, g1, g2,
+                y_out, g_out, di_out, dr_out, dp_out, da_ref, s_gain, s_bias, s_out, s_in, s_back,
+                wqkv, wo, win, wback, dj, dx, gb, slope_b, resid_b, di_b, dr_b, dp_b, da_b,
+                w_sem, in_sem, out_sem, g_sem, x_send, x_recv, *sems):
+    section, dp, seq, core = place()
+    sibling = (section, dp + 1 - 2 * core, seq)
+    across = (1 - section, dp, seq)
+    tokens, width = x_ref.shape
+    steps = tokens // TOK
+    loads = [pltpu.make_async_copy(a, b, w_sem.at[n]) for n, (a, b) in enumerate(
+        ((wqkv_in, wqkv), (wback_in, wback), (win_in, win), (wo_in, wo)))]
+    loads[0].start()
+
+    def kept(i):
+        return [pltpu.make_async_copy(a.at[chunk(i)], b.at[chunk(i)], in_sem.at[n, i])
+                for n, (a, b) in enumerate(((slope_in, slope_b), (resid_in, resid_b)))]
+
+    def last(i):
+        return pltpu.make_async_copy(g_in.at[chunk(i)], gb.at[chunk(i)], g_sem.at[i])
+
+    greet(across, *column_mates(section, dp, seq, core))
+    to_tokens = ToTokens((dq_ref, dk_ref, dv_ref), dj, tokens, width, sems[:3], core, sibling)
+    to_heads = ToHeads(da_b, (da_ref,), tokens, width, sems[3:6], core, sibling)
+    blocks = Blocks(y_ref, y_out, False, sems[6:9], section, dp, seq, core)
+
+    @pl.loop(0, steps)
+    def _(i):
+        to_tokens.start(i)
+
+    sums = (s_gain, s_bias, s_out, s_in, s_back)
+    for s in sums:
+        s[...] = jnp.zeros_like(s)
+
+    def passed(i):
+        return remote(dx.at[chunk(i)], gb.at[chunk(i)], x_send.at[i], x_recv.at[i], across)
+
+    def results(i):
+        return [pltpu.make_async_copy(b.at[chunk(i)], o.at[chunk(i)], out_sem.at[n, i])
+                for n, (b, o) in enumerate(((gb, g_out), (di_b, di_out), (dr_b, dr_out), (dp_b, dp_out)))]
+
+    loads[0].wait()
+
+    @pl.loop(0, steps)
+    def _(i):
+        to_tokens.wait(i)
+
+        @pl.when(i == 0)
+        def _():
+            for load in loads[1:]:
+                load.start()
+
+        for copy in kept(i):
+            copy.start()
+
+        @pl.when(section == 1)
+        def _():
+            last(i).start()
+            dx[chunk(i), :] = input_back(i, dj, dr_ref, x_ref, wqkv, g1, None)
+            passed(i).start()
+
+    blocks.start()
+
+    for load in loads[1:]:
+        load.wait()
+
+    @pl.loop(0, steps)
+    def _(i):
+        for copy in kept(i):
+            copy.wait()
+
+        @pl.when(section == 0)
+        def _():
+            passed(i).wait_recv()
+
+        @pl.when(section == 1)
+        def _():
+            last(i).wait()
+
+        feed_back(i, gb[chunk(i), :], slope_b, resid_b, wo, win, wback, g2, di_b, dr_b, dp_b, da_b, sums)
+        to_heads.start(i)
+        for copy in results(i):
+            copy.start()
+
+    @pl.loop(0, steps)
+    def _(i):
+        to_tokens.wait_sent(i)
+        to_heads.wait(i)
+        for copy in results(i):
+            copy.wait()
+
+        @pl.when(section == 1)
+        def _():
+            passed(i).wait_send()
+
+    blocks.wait()
+
+
+def back_call(dq, dk, dv, dr, x, y, g, slope, resid, wqkv, wo, win, wback, g1, g2, each):
+    tokens, width = x.shape
+    hidden = win.shape[1]
+    steps = tokens // TOK
+    low, full, wide = sds(x.shape, BF16), sds(x.shape, F32), sds((tokens, hidden), BF16)
+    one = sds((8, width), F32)
+    buf = lambda s: pltpu.VMEM(s.shape, s.dtype)
+    return pl.pallas_call(
+        back_kernel,
+        in_specs=[ANY, ANY, ANY, VMEM, VMEM] + [ANY] * 8 + [VMEM, VMEM],
+        out_specs=[ANY] * 6 + [VMEM] * 5,
+        out_shape=[sds((each, tokens // each, width), BF16), low, wide, full, low, sds((2 * tokens, width // 2), BF16),
+                   one, one, one, sds((8, hidden), F32), one],
+        scratch_shapes=[buf(wqkv), buf(wo), buf(win), buf(wback), pltpu.VMEM((tokens, 3 * width), BF16),
+                        buf(low), buf(low), buf(wide), buf(full), buf(wide), buf(full), buf(low), buf(low),
+                        DMA((4,)), DMA((2, steps)), DMA((4, steps)), DMA((steps,)), DMA((steps,)), DMA((steps,))]
+        + swap_sems(3, steps) + swap_sems(1, steps) + block_sems(each),
+        compiler_params=pltpu.CompilerParams(collective_id=4, has_side_effects=True, vmem_limit_bytes=62 * MIB),
+        name="qkv_back_pass",
+    )(dq, dk, dv, dr, x, y, g, slope, resid, wqkv, wo, win, wback, g1, g2)
+
+
+def last_kernel(dq_ref, dk_ref, dv_ref, dr_ref, x_ref, w_in, gain,
+                dj_out, dx_out, s_gain, s_bias, s_q, s_v, w, dj, dxb, w_sem, out_sem, *sems):
+    section, dp, seq, core = place()
+    sibling = (section, dp + 1 - 2 * core, seq)
+    tokens, width = x_ref.shape
+    steps = tokens // TOK
+    load = pltpu.make_async_copy(w_in, w, w_sem)
+    load.start()
+    greet(sibling)
+    to_tokens = ToTokens((dq_ref, dk_ref, dv_ref), dj, tokens, width, sems, core, sibling)
+
+    def results(i):
+        return [pltpu.make_async_copy(b.at[chunk(i)], o.at[chunk(i)], out_sem.at[n, i])
+                for n, (b, o) in enumerate(((dj, dj_out), (dxb, dx_out)))]
+
+    @pl.loop(0, steps)
+    def _(i):
+        to_tokens.start(i)
+
+    sums = (s_gain, s_bias, s_q, s_v)
+    for s in sums:
+        s[...] = jnp.zeros_like(s)
+    load.wait()
+
+    @pl.loop(0, steps)
+    def _(i):
+        to_tokens.wait(i)
+        dxb[chunk(i), :] = input_back(i, dj, dr_ref, x_ref, w, gain, sums)
+        for copy in results(i):
+            copy.start()
+
+    @pl.loop(0, steps)
+    def _(i):
+        to_tokens.wait_sent(i)
+        for copy in results(i):
+            copy.wait()
+
+
+def last_call(dq, dk, dv, dr, x, w, gain):
+    tokens, width = x.shape
+    steps = tokens // TOK
+    joined = sds((tokens, 3 * width), BF16)
+    low, one = sds(x.shape, BF16), sds((8, width), F32)
+    buf = lambda s: pltpu.VMEM(s.shape, s.dtype)
+    return pl.pallas_call(
+        last_kernel,
+        in_specs=[ANY, ANY, ANY, VMEM, VMEM, ANY, VMEM],
+        out_specs=[ANY, ANY] + [VMEM] * 4,
+        out_shape=[joined, low] + [one] * 4,
+        scratch_shapes=[buf(w), buf(joined), buf(low), DMA, DMA((2, steps))] + swap_sems(3, steps),
+        compiler_params=pltpu.CompilerParams(collective_id=5, has_side_effects=True, vmem_limit_bytes=62 * MIB),
+        name="qkv_back",
+    )(dq, dk, dv, dr, x, w, gain)
+
+
+def core_rows(size, yy, core):
+    return span((2 * yy + core) * 4 * size, 4 * size)
+
+
+def attn_plan(width):
+    return [(width, width, 0, 0)] + [(width, width, 1, i * width) for i in range(3)]
+
+
+def piece(left, right, at, cols, out):
+    step = min(left.shape[0], 1024)
+
+    @pl.loop(0, left.shape[0] // step)
+    def _(r):
+        block = span(r * step, step)
+        out[block, :] = jnp.dot(left[block, :], right[:, at:at + cols], preferred_element_type=F32).astype(BF16)
+
+
+def ffn_grads_kernel(plan, left_in, right_in, out, left, right, *refs):
+    count = len(plan)
+    buf, rec = refs[:count], refs[count:2 * count]
+    load_sem, s_send, s_recv = refs[2 * count:]
+    section, dp, seq, core = place()
+    sibling = (section, dp + 1 - 2 * core, seq)
+    loads = [pltpu.make_async_copy(left_in, left, load_sem.at[0])]
+    loads += [pltpu.make_async_copy(right_in.at[:, at:at + cols], right.at[:, at:at + cols], load_sem.at[1 + p])
+              for p, (_, cols, at) in enumerate(plan)]
+    for load in loads:
+        load.start()
+    greet(sibling)
+
+    def sent(p, yy):
+        size = plan[p][0] // 16
+        return remote(buf[p].at[core_rows(size, yy, 1 - core)], rec[p].at[pl.ds(yy * 4 * size, 4 * size)],
+                      s_send.at[p, yy], s_recv.at[p, yy], sibling)
+
+    def add(p):
+        rows, cols, at = plan[p]
+        size = rows // 16
+        for yy in range(2):
+            sent(p, yy).wait_recv()
+            total = (buf[p][core_rows(size, yy, core), :].astype(F32)
+                     + rec[p][yy * 4 * size:(yy + 1) * 4 * size, :].astype(F32)).astype(BF16)
+            for zz in range(4):
+                out[zz * 2 * size + yy * size:zz * 2 * size + (yy + 1) * size, at:at + cols] = (
+                    total[zz * size:(zz + 1) * size, :])
+
+    loads[0].wait()
+    for p, (rows, cols, at) in enumerate(plan):
+        loads[1 + p].wait()
+        piece(left, right, at, cols, buf[p])
+        for yy in range(2):
+            sent(p, yy).start()
+        if p > 0:
+            add(p - 1)
+    add(count - 1)
+    for p in range(count):
+        for yy in range(2):
+            sent(p, yy).wait_send()
+
+
+def ffn_grads_call(number, left, right):
+    rows, columns = left.shape[0], right.shape[1]
+    cols = 768 if rows <= columns else 256
+    plan = [(rows, cols, at) for at in range(0, columns, cols)]
+    count = len(plan)
+    return pl.pallas_call(
+        partial(ffn_grads_kernel, plan),
+        in_specs=[ANY] * 2,
+        out_specs=VMEM,
+        out_shape=sds((rows // 2, columns), BF16),
+        scratch_shapes=[pltpu.VMEM(left.shape, BF16), pltpu.VMEM(right.shape, BF16)]
+        + [pltpu.VMEM((r, c), BF16) for r, c, _ in plan]
+        + [pltpu.VMEM((r // 2, c), BF16) for r, c, _ in plan]
+        + [DMA((1 + count,)), DMA((count, 2)), DMA((count, 2))],
+        compiler_params=pltpu.CompilerParams(collective_id=number, has_side_effects=True, vmem_limit_bytes=62 * MIB),
+        name="ffn_weight_grads",
+    )(left, right)
+
+
+def grads_kernel(n_small, *refs):
+    refs = list(refs)
+    lefts = [refs.pop(0) for _ in range(2)]
+    rights = [refs.pop(0) for _ in range(2)]
+    ffn_in = [refs.pop(0) for _ in range(2)]
+    dx = refs.pop(0)
+    sums = [refs.pop(0) for _ in range(n_small)]
+    outs = [refs.pop(0) for _ in range(2)]
+    ffn_out = [refs.pop(0) for _ in range(2)]
+    small_out, dx_out = refs.pop(0), refs.pop(0)
+    left_buf = [refs.pop(0) for _ in range(2)]
+    right_buf = [refs.pop(0) for _ in range(2)]
+    ffn_rec = [refs.pop(0) for _ in range(2)]
+    width, tokens = lefts[0].shape
+    plan = attn_plan(width)
+    buf1 = [refs.pop(0) for _ in plan]
+    rec1 = [refs.pop(0) for _ in plan]
+    rec2 = [refs.pop(0) for _ in plan]
+    rec3 = [refs.pop(0) for _ in plan]
+    small, small1, small2, small3 = [refs.pop(0) for _ in range(4)]
+    (load_sem, s1_send, s1_recv, s2_send, s2_recv, s3_send, s3_recv,
+     m_send, m_recv, f_send, f_recv) = refs[:11]
+
+    section, dp, seq, core = place()
+    y = dp // 2
+    sibling = (section, dp + 1 - 2 * core, seq)
+    across_y = (section, dp + 2 - 4 * y, seq)
+    along = [(section, dp, lax.rem(seq + t, 4)) for t in range(1, 4)]
+    count = len(plan)
+    loads = [[pltpu.make_async_copy(lefts[t], left_buf[t], load_sem.at[0, t]),
+              pltpu.make_async_copy(rights[t], right_buf[t], load_sem.at[1, t])] for t in range(2)]
+    for pair in loads:
+        for load in pair:
+            load.start()
+    greet(across_y, *column_mates(section, dp, seq, core))
+    blocks = Blocks(dx, dx_out, False, refs[11:14], section, dp, seq, core)
+    blocks.start()
+
+    def ffn_sent(n):
+        size = ffn_in[n].shape[0] // 2
+        return remote(ffn_in[n].at[span((1 - y) * size, size)], ffn_rec[n], f_send.at[n], f_recv.at[n], across_y)
+
+
+    size = width // 16
+
+    def half(yy):
+        return span(yy * 4 * size, 4 * size)
+
+    def first(p, yy):
+        return remote(buf1[p].at[core_rows(size, yy, 1 - core)], rec1[p].at[half(yy)],
+                      s1_send.at[p, yy], s1_recv.at[p, yy], sibling)
+
+    def second(p):
+        return remote(rec1[p].at[half(1 - y)], rec2[p], s2_send.at[p], s2_recv.at[p], across_y)
+
+    def third(p, t):
+        rows = span(y * 4 * size + lax.rem(seq + t, 4) * size, size)
+        return remote(rec1[p].at[rows], rec3[p].at[seq], s3_send.at[p, t - 1], s3_recv.at[p, t - 1], along[t - 1])
+
+    def third_got(p, t):
+        rows = span(y * 4 * size + seq * size, size)
+        return remote(rec1[p].at[rows], rec3[p].at[lax.rem(seq + 4 - t, 4)],
+                      s3_send.at[p, t - 1], s3_recv.at[p, t - 1], along[t - 1])
+
+    def reduce_core(p):
+        for yy in range(2):
+            first(p, yy).wait_recv()
+            total = buf1[p][core_rows(size, yy, core), :].astype(F32) + rec1[p][half(yy), :].astype(F32)
+            rec1[p][half(yy), :] = total.astype(BF16)
+        second(p).start()
+
+    def reduce_y(p):
+        second(p).wait_recv()
+        mine = half(y)
+        rec1[p][mine, :] = (rec1[p][mine, :].astype(F32) + rec2[p][...].astype(F32)).astype(BF16)
+        for t in range(1, 4):
+            third(p, t).start()
+
+    def reduce_z(p):
+        rows, cols, t_out, at = plan[p]
+        total = rec1[p][span(y * 4 * size + seq * size, size), :].astype(F32)
+        for t in range(1, 4):
+            third_got(p, t).wait_recv()
+            total = total + rec3[p][lax.rem(seq + 4 - t, 4)].astype(F32)
+        outs[t_out][:, at:at + cols] = total
+
+    line = 0
+    for s in sums:
+        row = jnp.sum(s[...], axis=0, keepdims=True)
+        for t in range(s.shape[1] // 128):
+            small[line:line + 1, :] = row[:, t * 128:(t + 1) * 128]
+            line += 1
+    v1 = remote(small, small1, m_send.at[0], m_recv.at[0], sibling)
+    v2 = remote(small, small2, m_send.at[1], m_recv.at[1], across_y)
+
+    def v3(t):
+        return remote(small, small3.at[t - 1], m_send.at[1 + t], m_recv.at[1 + t], along[t - 1])
+
+    v1.start()
+    v1.wait()
+    small[...] += small1[...]
+    v2.start()
+    ready = set()
+    for p, (rows, cols, t, at) in enumerate(plan):
+        if t not in ready:
+            ready.add(t)
+            for load in loads[t]:
+                load.wait()
+        piece(left_buf[t], right_buf[t], at, cols, buf1[p])
+        for yy in range(2):
+            first(p, yy).start()
+        if p > 0:
+            reduce_core(p - 1)
+        if p == 1:
+            v2.wait()
+            small[...] += small2[...]
+            for t in range(1, 4):
+                v3(t).start()
+    reduce_core(count - 1)
+    for n in range(2):
+        ffn_sent(n).start()
+    for p in range(count):
+        reduce_y(p)
+    for n in range(2):
+        ffn_sent(n).wait_recv()
+        rows = ffn_in[n].shape[0] // 2
+        ffn_out[n][...] = ffn_in[n][span(y * rows, rows), :].astype(F32) + ffn_rec[n][...].astype(F32)
+    for t in range(1, 4):
+        v3(t).wait()
+    small_out[...] = small[...] + small3[0] + small3[1] + small3[2]
+    for p in range(count):
+        reduce_z(p)
+
+    for p in range(count):
+        for yy in range(2):
+            first(p, yy).wait_send()
+        second(p).wait_send()
+        for t in range(1, 4):
+            third(p, t).wait_send()
+    for n in range(2):
+        ffn_sent(n).wait_send()
+    blocks.wait()
+
+
+def grads_call(att_t, norm_t, d_proj, d_joined, ffn, dx, sums, each):
+    width, tokens = att_t.shape
+    plan = attn_plan(width)
+    count = len(plan)
+    lines = sum(s.shape[1] for s in sums) // 128
+    vec = pltpu.VMEM((lines, 128), F32)
+    halves = [(f.shape[0] // 2, f.shape[1]) for f in ffn]
+    return pl.pallas_call(
+        partial(grads_kernel, len(sums)),
+        in_specs=[ANY] * 4 + [VMEM] * 2 + [ANY] + [VMEM] * len(sums),
+        out_specs=[VMEM] * 5 + [ANY],
+        out_shape=[sds((width // 16, width), F32), sds((width // 16, 3 * width), F32)]
+        + [sds(h, F32) for h in halves]
+        + [sds((lines, 128), F32), sds((each, tokens // each, width), BF16)],
+        scratch_shapes=(
+            [pltpu.VMEM(a.shape, BF16) for a in (att_t, norm_t, d_proj, d_joined)]
+            + [pltpu.VMEM(h, BF16) for h in halves]
+            + [pltpu.VMEM((r, c), BF16) for r, c, *_ in plan]
+            + [pltpu.VMEM((r // 2, c), BF16) for r, c, *_ in plan]
+            + [pltpu.VMEM((r // 4, c), BF16) for r, c, *_ in plan]
+            + [pltpu.VMEM((4, r // 16, c), BF16) for r, c, *_ in plan]
+            + [vec, vec, vec, pltpu.VMEM((3, lines, 128), F32)]
+            + [DMA((2, 2)), DMA((count, 2)), DMA((count, 2)), DMA((count,)), DMA((count,)),
+               DMA((count, 3)), DMA((count, 3)), DMA((5,)), DMA((5,)), DMA((2,)), DMA((2,))]
+            + block_sems(each)),
+        compiler_params=pltpu.CompilerParams(collective_id=8, has_side_effects=True, vmem_limit_bytes=62 * MIB),
+        name="weight_grads",
+    )(att_t, norm_t, d_proj, d_joined, *ffn, dx, *sums)
+
+
+def swap_cores(x):
+    size = lax.axis_size("dp")
+    return lax.ppermute(x, "dp", [(i, i ^ 1) for i in range(size)])
+
+
+def on_device_rows(cell_tokens, cell_lengths, out_grad, *raw_weights):
+    (gain1, bias1, wqkv, qb, vb, wo, bo, gain2, bias2, win, bi, wback, bb) = tuple(
+        (w if w.ndim == 2 else w[0] for w in raw_weights)
+    )
+    each, local, width = cell_tokens.shape
+    row_length = local * lax.axis_size("seq")
+    core = lax.axis_index("dp") % 2
+    z = lax.axis_index("seq")
+
+    lengths = jnp.where(z // each == core, cell_lengths, swap_cores(cell_lengths))
+    lengths = lax.dynamic_index_in_dim(lengths, z % each, 0, keepdims=False)
+    fq, fk, lo, hi = segment_terms(lengths, row_length)
+
+    x, q, k, v = first_call(cell_tokens, wqkv, gain1, bias1, qb, vb)
+    o, _ = attn_fwd(lo, hi, q, k, v, fq, fk)
+    x, g, norm_t, q, k, v = pass_call(
+        o, x, out_grad, wo, win, wback, wqkv, (bo, gain2, bias2, bi, bb, gain1, bias1, qb, vb))
+    o, lse = attn_fwd(lo, hi, q, k, v, fq, fk)
+    y, resid, slope, att_t, c_t, act_t, dr, do = turn_call(o, x, g, wo, win, wback, (bo, gain2, bias2, bi, bb))
+
+    dq, dk, dv = attn_bwd(lo, hi, q, k, v, do, o, lse, fq, fk)
+    outputs, g, di, dr, dp, do, s_gain2, s_bias2, s_out, s_in, s_back = back_call(
+        dq, dk, dv, dr, x, y, g, slope, resid, wqkv, wo, win, wback, gain1, gain2, each)
+    ffn = [ffn_grads_call(6, c_t, di), ffn_grads_call(7, act_t, g)]
+    ffn = [lax.psum_scatter(w, "seq", scatter_dimension=0, tiled=True) for w in ffn]
+    dq, dk, dv = attn_bwd(lo, hi, q, k, v, do, o, lse, fq, fk)
+    dj, dx, s_gain1, s_bias1, s_q, s_v = last_call(dq, dk, dv, dr, x, wqkv, gain1)
+    sums = (s_gain1, s_bias1, s_q, s_v, s_out, s_gain2, s_bias2, s_in, s_back)
+    g_out, g_qkv, g_in, g_back, small, in_grads = grads_call(att_t, norm_t, dp, dj, ffn, dx, sums, each)
+
+    flat = small.reshape(-1)
+    parts = lax.axis_size("dp") * lax.axis_size("seq")
+    owner = lax.axis_index("dp") * lax.axis_size("seq") + z
+    shares, at = [], 0
+    for s in sums:
+        size = s.shape[1] // parts
+        shares.append(lax.dynamic_slice_in_dim(flat, at + owner * size, size))
+        at += s.shape[1]
+    return (
+        outputs[None],
+        in_grads.astype(F32)[None],
+        shares[0][None],
+        shares[1][None],
+        g_qkv[None],
+        shares[2][None],
+        shares[3][None],
+        g_out[None],
+        shares[4][None],
+        shares[5][None],
+        shares[6][None],
+        g_in[None],
+        shares[7][None],
+        g_back[None],
+        shares[8][None],
+    )
+
+
+def either_plan(cell_tokens, *others):
+    one_chip = lax.axis_size("dp") % 2 == 0 and lax.axis_size("seq") == 2 * cell_tokens.shape[0] and lax.axis_size("section") == 2 and lax.axis_size("dp") == lax.axis_size("seq") == 4
+    return (on_device_rows if one_chip else on_device)(cell_tokens, *others)
+
+
 def solution(mesh):
     in_specs = (
         P("dp", "seq", None),
@@ -364,5 +1663,5 @@
         P("section", ("dp", "seq")),
     )
     return jax.shard_map(
-        on_device, mesh=mesh, in_specs=in_specs, out_specs=out_specs, check_vma=False
-    )
+        either_plan, mesh=mesh, in_specs=in_specs, out_specs=out_specs, check_vma=False
+    )

time: 2250 us -> 515 us (0.23)
  waiting for transfers between devices: 1040 us -> 11.2 us
  matrix products: 782 us -> 0 us
  Pallas kernels: 0 us -> 472 us
  other arithmetic: 189 us -> 5.79 us
  local copies, waits for them, and re-layouts: 113 us -> 7.06 us
  blocking collectives: 60.4 us -> 0 us
    dot_general x60 -> x0, matrix products: 636 us -> none  [the longest x6 117 us: attend(): jnp.einsum('hqk,khe->qhe', low_probs, split_heads(values_all), preferred_...]
    all_gather x12 -> x0, waiting for transfers between devices: 548 us -> none  [the longest x3 174 us: forward_tick(): lax.all_gather(keys_out, 'seq', axis=0, tiled=True)]
    pallas_call x0 -> x12, Pallas kernels: none -> 472 us  [the longest x2 126 us: attn_bwd(): pl.pallas_call(bwd_kernel, grid_spec=pltpu.PrefetchScalarGridSpec(num_sca...]
    reduce_scatter x10 -> x2, waiting for transfers between devices: 412 us -> 11.1 us  [on_device_rows(): lax.psum_scatter(w, 'seq', scatter_dimension=0, tiled=True)]
    sub x6 -> x0, matrix products: 147 us -> none  [softmax_parts(): raised = jnp.exp(scores - highest[..., None])]
    convert_element_type x14 -> x1, other arithmetic: 147 us -> 1.35 us  [segment_terms(): fk = jnp.where(used & ~hot, 1.0, 0.0).astype(BF16)]
    ppermute x6 -> x1, waiting for transfers between devices: 82.6 us -> 0.01 us  [swap_cores(): return lax.ppermute(x, 'dp', [(i, i ^ 1) for i in range(size)])]
    unnamed x1 -> x0, blocking collectives: 60.4 us -> none
  transfers between devices with their start and end apart: 28 -> 3, of which waited for: 24 -> 1; matrix products, arithmetic and copies ran while one was open for 24% -> 0% of each run, Pallas kernels for 0% -> 23%
where the time goes in v1:
time: 515 us; the launch traced here: 511 us
  Pallas kernels  472 us (92%)
  between operations  14.5 us (3%)
  waiting for transfers between devices  11.2 us (2%)
  local copies, waits for them, and re-layouts  7.06 us (1%)
  other arithmetic  5.79 us (1%)
    pallas_call x2, Pallas kernels, attn_bwd(): pl.pallas_call(bwd_kernel, grid_spec=pltpu.PrefetchScalarGridSpec(num_sca...  126 us
    pallas_call x1, Pallas kernels, grads_call(): pl.pallas_call(partial(grads_kernel, len(sums)), in_specs=[ANY] * 4 + [VM...  69.9 us
    pallas_call x2, Pallas kernels, attn_fwd(): pl.pallas_call(fwd_kernel, grid_spec=pltpu.PrefetchScalarGridSpec(num_sca...  63.1 us
    pallas_call x1, Pallas kernels, back_call(): pl.pallas_call(back_kernel, in_specs=[ANY, ANY, ANY, VMEM, VMEM] + [ANY]...  55 us
    pallas_call x1, Pallas kernels, pass_call(): pl.pallas_call(pass_kernel, in_specs=[ANY, VMEM, ANY, ANY, ANY, ANY, ANY]...  45.5 us
    pallas_call x1, Pallas kernels, turn_call(): pl.pallas_call(turn_kernel, in_specs=[ANY, VMEM, VMEM, ANY, ANY, ANY] + [...  43.9 us
    pallas_call x1, Pallas kernels, first_call(): pl.pallas_call(first_kernel, in_specs=[ANY, ANY] + [VMEM] * 4, out_specs=...  30.6 us
    pallas_call x2, Pallas kernels, ffn_grads_call(): pl.pallas_call(partial(ffn_grads_kernel, plan), in_specs=[ANY] * 2, out_s...  25.8 us
  transfers between devices with their start and end apart: 3, of which 1 were waited for; matrix products, arithmetic and copies ran while one was open for 0% of the time, Pallas kernels for 23%

profile of v1, /device:TPU:0, one launch (start us, length us, event | category | flops | bytes accessed | tf_op | source)
XLA Modules:
  0.0 511.0 jit_solution(5774219878493239507)
XLA Ops:
  7.2 0.0 reduce-scatter.5.cloned.1.call-start
  7.2 0.5 collective-permute-start
  7.8 30.6 %rows_qkv.1 = (bf16[1024,768]{1,0:T(8,128)(2,1)}, bf16[2048,384]{1,0:T(8,128)(2,1)}, bf16[2048,384]{1,0:T(8,128)(2,1)}, bf16[2048,384]{1,0:T(8,128)(2,1)}) custom-call(bf16[2,512,768]{2,1,0:T(8,128)(2,1)} %x_ref.1, bf16[768,2304]{1,0:T(8,128)(2,1)} %bitcast.40, bf16[1,768]{1,0:T(2,128)(2,1)} %gain.3, bf16[1,768]{1,0:T(2,128)(2,1)} %b1.1, bf16[1,768]{1,0:T(2,128)(2,1)} %qb.3, ...), custom_call_target="tpu_custom_call" | custom-call | tf_op jit(solution)/shard_map/rows_qkv/pallas_call | solution.py:867
  38.4 0.1 select_reduce_fusion
  38.6 0.2 select_reduce_fusion.1
  38.8 0.2 select_reduce_fusion.2
  39.0 0.5 and_select_fusion
  39.5 1.3 select_convert_fusion
  40.8 31.6 %attn_fwd.2 = (bf16[2048,384]{1,0:T(8,128)(2,1)}, f32[3,8,2048]{2,1,0:T(8,128)}) custom-call(s32[8]{0:T(128)} %get-tuple-element.126.lo_ref, s32[8]{0:T(128)} %get-tuple-element.125.hi_ref, bf16[2048,384]{1,0:T(8,128)(2,1)} %get-tuple-element.65.q_ref, bf16[2048,384]{1,0:T(8,128)(2,1)} %get-tuple-element.66.k_ref, ...), custom_call_target="tpu_custom_call" | custom-call | tf_op jit(solution)/shard_map/attn_fwd/pallas_call | solution.py:417
  72.4 45.5 %ffn_pass_qkv.1 = (bf16[1024,768]{1,0:T(8,128)(2,1)}, bf16[1024,768]{1,0:T(8,128)(2,1)}, bf16[768,1024]{1,0:T(8,128)(2,1)}, bf16[2048,384]{1,0:T(8,128)(2,1)}, b...) custom-call(bf16[2048,384]{1,0:T(8,128)(2,1)} %get-tuple-element.68.o_ref, ...), custom_call_target="tpu_custom_call" | custom-call | tf_op jit(solution)/shard_map/ffn_pass_qkv/pallas_call | solution.py:1034
  117.9 31.5 %attn_fwd.3 = (bf16[2048,384]{1,0:T(8,128)(2,1)}, f32[3,8,2048]{2,1,0:T(8,128)}) custom-call(s32[8]{0:T(128)} %get-tuple-element.126.lo_ref, s32[8]{0:T(128)} %get-tuple-element.125.hi_ref, bf16[2048,384]{1,0:T(8,128)(2,1)} %get-tuple-element.70.q_ref, bf16[2048,384]{1,0:T(8,128)(2,1)} %get-tuple-element.71.k_ref, ...), custom_call_target="tpu_custom_call" | custom-call | tf_op jit(solution)/shard_map/attn_fwd/pallas_call | solution.py:417
  149.5 43.9 %ffn_turn.1 = (bf16[1024,768]{1,0:T(8,128)(2,1)}, f32[1024,768]{1,0:T(8,128)}, bf16[1024,3072]{1,0:T(8,128)(2,1)}, bf16[768,1024]{1,0:T(8,128)(2,1)}, bf16[768,1...) custom-call(bf16[2048,384]{1,0:T(8,128)(2,1)} %get-tuple-element.73.o_ref, ...), custom_call_target="tpu_custom_call" | custom-call | tf_op jit(solution)/shard_map/ffn_turn/pallas_call | solution.py:1108
  193.4 63.1 %attn_bwd.2 = (bf16[2048,384]{1,0:T(8,128)(2,1)}, bf16[2048,384]{1,0:T(8,128)(2,1)}, bf16[2048,384]{1,0:T(8,128)(2,1)}) custom-call(s32[8]{0:T(128)} %get-tuple-element.126.lo_ref, s32[8]{0:T(128)} %get-tuple-element.125.hi_ref, bf16[2048,384]{1,0:T(8,128)(2,1)} %get-tuple-element.70.q_ref, bf16[2048,384]{1,0:T(8,128)(2,1)} %get-tuple-element.71.k_ref, ...), custom_call_target="tpu_custom_call" | custom-call | tf_op jit(solution)/shard_map/attn_bwd/pallas_call | solution.py:523
  256.5 55.0 %qkv_back_pass.1 = (bf16[2,512,768]{2,1,0:T(8,128)(2,1)}, bf16[1024,768]{1,0:T(8,128)(2,1)}, bf16[1024,3072]{1,0:T(8,128)(2,1)}, f32[1024,768]{1,0:T(8,128)}, bf...) custom-call(bf16[2048,384]{1,0:T(8,128)(2,1)} %get-tuple-element.78., ...), custom_call_target="tpu_custom_call" | custom-call | tf_op jit(solution)/shard_map/qkv_back_pass/pallas_call | solution.py:1239
  311.5 12.9 %ffn_weight_grads.3 = bf16[1536,768]{1,0:T(8,128)(2,1)} custom-call(bf16[3072,1024]{1,0:T(8,128)(2,1)} %get-tuple-element.97.left_in, bf16[1024,768]{1,0:T(8,128)(2,1)} %get-tuple-element.98.right_in), custom_call_target="tpu_custom_call" | custom-call | tf_op jit(solution)/shard_map/ffn_weight_grads/pallas_call | solution.py:1374
  324.4 0.0 reduce-scatter.5.cloned.1.call-update
  324.4 0.0 reduce-scatter.3.cloned.1.call-start
  324.5 12.9 %ffn_weight_grads.2 = bf16[384,3072]{1,0:T(8,128)(2,1)} custom-call(bf16[768,1024]{1,0:T(8,128)(2,1)} %get-tuple-element.95.left_in, bf16[1024,3072]{1,0:T(8,128)(2,1)} %get-tuple-element.96.right_in), custom_call_target="tpu_custom_call" | custom-call | tf_op jit(solution)/shard_map/ffn_weight_grads/pallas_call | solution.py:1374
  337.4 62.9 %attn_bwd.3 = (bf16[2048,384]{1,0:T(8,128)(2,1)}, bf16[2048,384]{1,0:T(8,128)(2,1)}, bf16[2048,384]{1,0:T(8,128)(2,1)}) custom-call(s32[8]{0:T(128)} %get-tuple-element.126.lo_ref, s32[8]{0:T(128)} %get-tuple-element.125.hi_ref, bf16[2048,384]{1,0:T(8,128)(2,1)} %get-tuple-element.70.q_ref, bf16[2048,384]{1,0:T(8,128)(2,1)} %get-tuple-element.71.k_ref, ...), custom_call_target="tpu_custom_call" | custom-call | tf_op jit(solution)/shard_map/attn_bwd/pallas_call | solution.py:523
  400.3 12.1 %qkv_back.1 = (bf16[1024,2304]{1,0:T(8,128)(2,1)}, bf16[1024,768]{1,0:T(8,128)(2,1)}, f32[8,768]{1,0:T(8,128)}, f32[8,768]{1,0:T(8,128)}, f32[8,768]{1,0:T(8,128)}, /*index=5*/f32[8,768]{1,0:T(8,128)}) custom-call(bf16[2048,384]{1,0:T(8,128)(2,1)} %get-tuple-element.90.dq_ref, bf16[2048,384]{1,0:T(8,128)(2,1)} %get-tuple-element.91.dk_ref, ...), custom_call_target="tpu_custom_call" | custom-call | tf_op jit(solution)/shard_map/qkv_back/pallas_call | solution.py:1298
  412.4 0.0 reduce-scatter.5.cloned.1.call-done.refs_5_
  412.5 11.1 %reduce-scatter.3.cloned.1.call-done.refs_4_ = bf16[96,3072]{1,0:T(8,128)(2,1)} async-done(((bf16[384,3072]{1,0:T(8,128)(2,1)}), bf16[96,3072]{1,0:T(8,128)(2,1)}) %reduce-scatter.3.cloned.1.call-update) | async-done | bytes 589840 | tf_op jit(solution)/shard_map/reduce_scatter | solution.py:1591
  423.6 69.9 %weight_grads.1 = (f32[48,768]{1,0:T(8,128)}, f32[48,2304]{1,0:T(8,128)}, f32[48,3072]{1,0:T(8,128)}, f32[192,768]{1,0:T(8,128)}, f32[72,128]{1,0:T(8,128)}, /*index=5*/bf16[2,512,768]{2,1,0:T(8,128)(2,1)}) custom-call(bf16[768,1024]{1,0:T(8,128)(2,1)} %get-tuple-element.86.refs_0_, bf16[768,1024]{1,0:T(8,128)(2,1)} %get-tuple-element.87.refs_1_, ...), custom_call_target="tpu_custom_call" | custom-call | tf_op jit(solution)/shard_map/weight_grads/pallas_call | solution.py:1539
  493.5 3.4 bitcast_convert_fusion
  496.9 1.3 dynamic_slice.39
  498.2 1.4 dynamic-slice_bitcast_fusion
  499.7 1.1 copy.36
  500.8 0.1 copy-done.3
  500.9 0.8 copy.37
  501.7 0.7 copy.38
  502.3 0.8 copy.39
  503.1 0.8 copy.40
  (22 shorter events, 0.1 us)
Async XLA Ops:
  7.2 405.3 %reduce-scatter.5.cloned.1.call-start = ((), (), s32[]{:S(2)}) async-start(), calls=%async_computation.3 | async-start | bytes 2949120 | tf_op jit(solution)/shard_map/reduce_scatter | solution.py:1591
  7.2 31.2 %collective-permute-start = (s32[2,16]{1,0:T(2,128)}, s32[2,16]{1,0:T(2,128)S(1)}, u32[]{:S(2)}, u32[]{:S(2)}) collective-permute-start(s32[2,16]{1,0:T(2,128)} %param.17), channel_id=1, source_target_pairs={{0,4},{4,0},{8,12},{12,8},{1,5},{5,1},{9,13},{13,9},{2,6},{6,2},{1... | collective-permute-start | bytes 392 | tf_op jit(solution)/shard_map/ppermute | solution.py:1564
  7.8 30.6 %copy-start.5 = (s32[2,16]{1,0:T(2,128)S(1)}, s32[2,16]{1,0:T(2,128)}, u32[]{:S(2)}) copy-start(s32[2,16]{1,0:T(2,128)} %param.17) | copy-start | bytes 388
  324.4 99.2 %reduce-scatter.3.cloned.1.call-start = ((), (), s32[]{:S(2)}) async-start(), calls=%async_computation.2 | async-start | bytes 2949120 | tf_op jit(solution)/shard_map/reduce_scatter | solution.py:1591
  493.4 6.2 %copy-start = (bf16[2,512,768]{2,1,0:T(8,128)(2,1)S(1)}, bf16[2,512,768]{2,1,0:T(8,128)(2,1)}, u32[]{:S(2)}) copy-start(bf16[2,512,768]{2,1,0:T(8,128)(2,1)} %get-tuple-element.85) | copy-start | bytes 4718596
  499.7 1.2 copy-start.3
  499.7 2.0 copy-start.4
  499.7 2.6 copy-start.2
  500.9 2.2 copy-start.1
Sparse Core Ops, SparseCore 0:
  324.5 49.1 reduce-scatter.4
  376.0 47.5 reduce-scatter.2
